TPU v7x, 32 devices: a whole 2x2x4 slice. The times are simulated.
32 devices in a mesh: depth: 4 (over y, core), lat: 8 (over z, x).
Axes of the slice: x: 2, y: 2, z: 4, core: 2. Of those that a mesh axis runs over, the one named last changes fastest.
Arguments:
- volume: float32 [128, 128, 128], P('depth', 'lat'), may hold values from -6 to 6
Outputs:
- diffused: float32 [128, 128, 128], P('depth', 'lat')
All inputs are finite; a program needn't handle non-finite values.
Results may differ from a plain program's by a relative error of at most 0.0003.
Values sent between devices are 32-bit elements; how exact they have to be, the bound alone decides.
A program may use at most 64 MiB of HBM per device.

v0:
```python
import jax
import jax.numpy as jnp
from jax import lax
from jax.sharding import PartitionSpec as P

TAU = 300.0
LAMBDA = 0.5


def with_halo(block, sides, width):
    for axis, dim in sides:
        count = lax.axis_size(axis)
        forward = [(i, i + 1) for i in range(count - 1)]
        backward = [(target, source) for source, target in forward]
        low = lax.ppermute(
            lax.slice_in_dim(block, block.shape[dim] - width, None, axis=dim), axis, forward
        )
        high = lax.ppermute(lax.slice_in_dim(block, 0, width, axis=dim), axis, backward)
        block = jnp.concatenate([low, block, high], axis=dim)
    return block


def conductance(diff):
    ratio = diff / LAMBDA
    return 1.0 / (1.0 + ratio * ratio)


def shifted(field, shift_by, axis, fill):
    length = field.shape[axis]
    widths = [(0, 0)] * field.ndim
    if shift_by > 0:
        widths[axis] = (shift_by, 0)
        padded = jnp.pad(field, widths, constant_values=fill)
        return lax.slice_in_dim(padded, 0, length, axis=axis)
    widths[axis] = (0, -shift_by)
    padded = jnp.pad(field, widths, constant_values=fill)
    return lax.slice_in_dim(padded, -shift_by, length - shift_by, axis=axis)


def smooth_padded(field, axis):
    return 0.25 * (shifted(field, 1, axis, 0.0) + 2.0 * field + shifted(field, -1, axis, 0.0))


def smooth_valid(field, axis):
    length = field.shape[axis]
    before = lax.slice_in_dim(field, 0, length - 2, axis=axis)
    middle = lax.slice_in_dim(field, 1, length - 1, axis=axis)
    after = lax.slice_in_dim(field, 2, length, axis=axis)
    return 0.25 * (before + 2.0 * middle + after)


def edge_mask(count, index, total, axis):
    edges = index * count + jnp.arange(count + 1, dtype=jnp.int32) - 1
    valid = jnp.logical_and(edges >= 0, edges <= count * total - 2).astype(jnp.float32)
    shape = [1, 1, 1]
    shape[axis] = count + 1
    return valid.reshape(shape)


def cyclic_solve(lower, diag, upper, sources, axis):
    length = diag.shape[axis]
    offset = 1
    while offset < length:
        low_prev = shifted(lower, offset, axis, 0.0)
        diag_prev = shifted(diag, offset, axis, 1.0)
        up_prev = shifted(upper, offset, axis, 0.0)
        low_next = shifted(lower, -offset, axis, 0.0)
        diag_next = shifted(diag, -offset, axis, 1.0)
        up_next = shifted(upper, -offset, axis, 0.0)
        left_factor = -lower / diag_prev
        right_factor = -upper / diag_next
        sources = tuple(
            (
                source
                + left_factor * shifted(source, offset, axis, 0.0)
                + right_factor * shifted(source, -offset, axis, 0.0)
                for source in sources
            )
        )
        diag = diag + left_factor * up_prev + right_factor * low_next
        lower = left_factor * low_prev
        upper = right_factor * up_next
        offset = offset * 2
    return tuple((source / diag for source in sources))


def line_coefficients(forward, axis):
    lower = -3.0 * TAU * shifted(forward, 1, axis, 0.0)
    upper = -3.0 * TAU * forward
    return (lower, 1.0 - lower - upper, upper)


def local_spike(edges, field, axis):
    count = field.shape[axis]
    inner_lower = -3.0 * TAU * lax.slice_in_dim(edges, 0, count, axis=axis)
    inner_upper = -3.0 * TAU * lax.slice_in_dim(edges, 1, count + 1, axis=axis)
    diag = 1.0 - inner_lower - inner_upper
    shape = [1, 1, 1]
    shape[axis] = count
    position = jnp.arange(count, dtype=jnp.int32).reshape(shape)
    is_first = position == 0
    is_last = position == count - 1
    lower = jnp.where(is_first, 0.0, inner_lower)
    upper = jnp.where(is_last, 0.0, inner_upper)
    left_source = jnp.where(is_first, inner_lower, 0.0)
    right_source = jnp.where(is_last, inner_upper, 0.0)
    particular, left_spike, right_spike = cyclic_solve(
        lower, diag, upper, (field, left_source, right_source), axis
    )
    ends = []
    for solved in (particular, left_spike, right_spike):
        ends.append(lax.index_in_dim(solved, 0, axis, keepdims=False))
        ends.append(lax.index_in_dim(solved, count - 1, axis, keepdims=False))
    return (particular, left_spike, right_spike, jnp.stack(ends, axis=0)[None])


def reduced_solve(gathered):

    def sweep_down(carry, block):
        chain_prev, carry_last = carry
        first_val = block[0]
        last_val = block[1]
        left_first = block[2]
        left_last = block[3]
        right_first = block[4]
        right_last = block[5]
        pivot = 1.0 - left_first * chain_prev
        result_first = (first_val - left_first * carry_last) / pivot
        result_last = last_val - left_last * carry_last + left_last * chain_prev * result_first
        factor_first = right_first / pivot
        chain_new = right_last + left_last * chain_prev * factor_first
        return ((chain_new, result_last), (factor_first, chain_new, result_first, result_last))

    zero_lines = jnp.zeros_like(gathered[0, 0])
    _, factors = lax.scan(sweep_down, (zero_lines, zero_lines), gathered)

    def sweep_up(first_later, block):
        factor_first, chain_new, result_first, result_last = block
        first_here = result_first - factor_first * first_later
        last_here = result_last - chain_new * first_later
        return (first_here, (first_here, last_here))

    _, (firsts, lasts) = lax.scan(sweep_up, zero_lines, factors, reverse=True)
    return (firsts, lasts)


def spike_finish(particular, left_spike, right_spike, firsts, lasts, index, total, axis):
    last_prev = lax.dynamic_index_in_dim(lasts, jnp.maximum(index - 1, 0), 0, keepdims=False)
    first_next = lax.dynamic_index_in_dim(
        firsts, jnp.minimum(index + 1, total - 1), 0, keepdims=False
    )
    return (
        particular
        - left_spike * jnp.expand_dims(last_prev, axis)
        - right_spike * jnp.expand_dims(first_next, axis)
    )


def shards(volume):
    depth_total = lax.axis_size("depth")
    depth_index = lax.axis_index("depth")
    lat_total = lax.axis_size("lat")
    lat_index = lax.axis_index("lat")
    planes, rows, columns = volume.shape
    padded = with_halo(volume, (("depth", 0), ("lat", 1)), 2)
    smoothed = smooth_padded(padded, 2)
    smoothed = smooth_valid(smoothed, 1)
    smoothed = smooth_valid(smoothed, 0)
    core = smoothed[1:-1, 1:-1]
    cond_x = jnp.pad(conductance(core[:, :, 1:] - core[:, :, :-1]), ((0, 0), (0, 0), (0, 1)))
    band_y = smoothed[1:-1]
    cond_y = conductance(band_y[:, 1:] - band_y[:, :-1]) * edge_mask(rows, lat_index, lat_total, 1)
    band_z = smoothed[:, 1:-1]
    cond_z = conductance(band_z[1:] - band_z[:-1]) * edge_mask(planes, depth_index, depth_total, 0)
    lower_x, diag_x, upper_x = line_coefficients(cond_x, 2)
    (solved_x,) = cyclic_solve(lower_x, diag_x, upper_x, (volume,), 2)
    field = lax.all_to_all(volume, "lat", split_axis=2, concat_axis=1, tiled=True)
    forward = lax.all_to_all(cond_y[:, 1:], "lat", split_axis=2, concat_axis=1, tiled=True)
    count, length, width = field.shape
    flat_field = jnp.transpose(field, (1, 0, 2)).reshape(length, count * width)
    flat_forward = jnp.transpose(forward, (1, 0, 2)).reshape(length, count * width)
    lower, diag, upper = line_coefficients(flat_forward, 0)
    (solved,) = cyclic_solve(lower, diag, upper, (flat_field,), 0)
    returned = jnp.transpose(solved.reshape(length, count, width), (1, 0, 2))
    solved_y = lax.all_to_all(returned, "lat", split_axis=1, concat_axis=2, tiled=True)
    part_z, left_z, right_z, ends_z = local_spike(cond_z, volume, 0)
    gathered_z = lax.all_gather(ends_z, "depth", axis=0, tiled=True)
    firsts_z, lasts_z = reduced_solve(gathered_z)
    solved_z = spike_finish(part_z, left_z, right_z, firsts_z, lasts_z, depth_index, depth_total, 0)
    return (solved_x + solved_y + solved_z) / 3.0


def solution(mesh):
    placed = (P("depth", "lat", None),)
    return jax.shard_map(
        shards, mesh=mesh, in_specs=placed, out_specs=P("depth", "lat", None), check_vma=False
    )
```

profile of v0, /device:TPU:0, one launch (start us, length us, event | category | flops | bytes accessed | tf_op | source)
XLA Modules:
  0.0 85.6 jit_solution(10166235461958541876)
XLA Ops:
  0.0 0.7 fusion.349
  0.7 1.3 %collective-permute-start.1 = (f32[2,16,128]{2,1,0:T(8,128)S(1)}, f32[2,16,128]{2,1,0:T(8,128)S(1)}, u32[]{:S(2)}, u32[]{:S(2)}) collective-permute-start(f32[2,16,128]{2,1,0:T(8,128)S(1)} %get-tuple-element.418), channel_id=1, source_target_pairs={{8,0},{16,8},{24,16},{9,1},{17,9},{25,17},{10,2},{18,10},{26,18},{... | collective-permute-start | bytes 49160 | tf_op jit(solution)/shard_map/ppermute | solution.py:18
  2.0 3.0 %collective-permute-start = (f32[2,16,128]{2,1,0:T(8,128)S(1)}, f32[2,16,128]{2,1,0:T(8,128)S(1)}, u32[]{:S(2)}, u32[]{:S(2)}) collective-permute-start(f32[2,16,128]{2,1,0:T(8,128)S(1)} %get-tuple-element.417), channel_id=1, source_target_pairs={{0,8},{8,16},{16,24},{1,9},{9,17},{17,25},{2,10},{10,18},{18,26},{... | collective-permute-start | bytes 49160 | tf_op jit(solution)/shard_map/ppermute | solution.py:15
  5.1 1.5 %copy.129 = f32[32,16,128]{0,1,2:T(8,128)S(1)} copy(f32[32,16,128]{2,1,0:T(8,128)} %param.5) | data formatting | bytes 524288 | tf_op args[0]
  6.5 1.2 %reshape.56 = f32[8,1,8192]{2,1,0:T(1,128)} reshape(f32[128,16,32]{2,1,0:T(8,128)S(1)} %bitcast.147) | data formatting | bytes 524288
  7.7 7.4 %all-to-all-start = ((f32[8,1,8192]{2,1,0:T(1,128)}), f32[8,1,8192]{2,1,0:T(1,128)S(1)}, u32[]{:S(2)}, u32[]{:S(2)}) async-start(f32[8,1,8192]{2,1,0:T(1,128)} %reshape.56), calls=%async_computation | async-start | bytes 524288 | tf_op jit(solution)/shard_map/all_to_all | solution.py:177
  15.2 3.9 %collective-permute-start.2 = (f32[36,2,128]{2,0,1:T(8,128)S(1)}, f32[36,2,128]{2,0,1:T(8,128)S(1)}, u32[]{:S(2)}, u32[]{:S(2)}) collective-permute-start(f32[36,2,128]{2,0,1:T(8,128)S(1)} %copy.153), channel_id=1, source_target_pairs={{0,1},{1,2},{2,3},{3,4},{4,5},{5,6},{6,7},{8,9},{9,10},{10,11},{11... | collective-permute-start | bytes 110600 | tf_op jit(solution)/shard_map/ppermute | solution.py:15
  19.4 1.3 %collective-permute-start.3 = (f32[36,2,128]{2,0,1:T(8,128)S(1)}, f32[36,2,128]{2,0,1:T(8,128)S(1)}, u32[]{:S(2)}, u32[]{:S(2)}) collective-permute-start(f32[36,2,128]{2,0,1:T(8,128)S(1)} %copy.154), channel_id=1, source_target_pairs={{1,0},{2,1},{3,2},{4,3},{5,4},{6,5},{7,6},{9,8},{10,9},{11,10},{12... | collective-permute-start | bytes 110600 | tf_op jit(solution)/shard_map/ppermute | solution.py:18
  20.6 1.5 %collective-permute-done.2 = f32[36,2,128]{2,0,1:T(8,128)S(1)} collective-permute-done((f32[36,2,128]{2,0,1:T(8,128)S(1)}, f32[36,2,128]{2,0,1:T(8,128)S(1)}, u32[]{:S(2)}, u32[]{:S(2)}) %collective-permute-start.2) | collective-permute-done | bytes 36896 | tf_op jit(solution)/shard_map/ppermute | solution.py:15
  22.2 3.5 %collective-permute-done.3 = f32[36,2,128]{2,0,1:T(8,128)S(1)} collective-permute-done((f32[36,2,128]{2,0,1:T(8,128)S(1)}, f32[36,2,128]{2,0,1:T(8,128)S(1)}, u32[]{:S(2)}, u32[]{:S(2)}) %collective-permute-start.3) | collective-permute-done | bytes 36896 | tf_op jit(solution)/shard_map/ppermute | solution.py:18
  25.7 0.3 fusion.10
  26.6 0.5 copy.133
  27.1 1.2 %reshape.58 = f32[8,1,8192]{2,1,0:T(1,128)} reshape(f32[128,16,32]{2,1,0:T(8,128)S(1)} %bitcast.145) | data formatting | bytes 524288
  28.6 0.3 fusion.70
  28.9 0.3 fusion.23
  29.5 0.3 fusion.34
  29.8 0.3 fusion.78
  31.1 0.5 copy-done.1
  31.7 5.6 %all-gather = f32[24,16,128]{2,1,0:T(8,128)S(1)} all-gather(f32[6,16,128]{2,1,0:T(8,128)S(1)} %constant_dynamic-update-slice_fusion.3), channel_id=2, replica_groups=mesh['depth'=4,'lat'=8] {'depth'}, dimensions={0}, use_global_device_ids=true | all-gather | bytes 245760 | tf_op jit(solution)/shard_map/all_gather | solution.py:187
  37.8 0.7 fusion.131
  38.6 0.7 fusion.136
  39.2 0.3 fusion.143
  39.6 0.6 fusion.148
  40.2 0.3 fusion.155
  40.6 0.6 fusion.160
  41.2 0.3 fusion.167
  41.5 5.0 %all-to-all-start.1 = ((f32[8,1,8192]{2,1,0:T(1,128)}), f32[8,1,8192]{2,1,0:T(1,128)}, u32[]{:S(2)}, u32[]{:S(2)}) async-start(f32[8,1,8192]{2,1,0:T(1,128)} %reshape.58), calls=%async_computation.1 | async-start | bytes 524288 | tf_op jit(solution)/shard_map/all_to_all | solution.py:178
  46.5 1.3 %fusion.172 = (f32[32,16,128]{2,0,1:T(8,128)}, f32[32,16,128]{2,0,1:T(8,128)S(1)}, f32[32,16,128]{2,0,1:T(8,128)S(1)}) fusion(f32[32,16,128]{2,0,1:T(8,128)S(1)} %get-tuple-element.323, f32[32,16,128]{2,0,1:T(8,128)S(1)} %fusion.167, f32[32,16,128]{2,0,1:T(8,128)S(1)} %get-tuple-element.324, f32[32,16,128]{2,0,1:T(8,128)S(1)} %fusion.155, ...), kind=kLoop, calls=%fused_computation.364 | loop fusion | flops 917504 | bytes 2097152 | tf_op jit(solution)/shard_map/add | solution.py:74
  47.8 0.3 fusion.179
  48.2 0.6 broadcast.571
  48.8 1.3 %reduce.1 = f32[8,8192]{1,0:T(8,128)S(1)} reduce(f32[8,1,8192]{2,1,0:T(1,128)S(1)} %all-to-all-done, f32[]{:T(128)} %broadcast.571), dimensions={1}, to_apply=%all_to_all.39.reduce_sub_computation | reduce | bytes 524292 | tf_op jit(solution)/shard_map/all_to_all | solution.py:177
  50.1 0.3 reshape.57
  50.4 0.3 copy.131
  50.7 1.2 %copy.132 = f32[128,32,16]{0,2,1:T(8,128)} copy(f32[128,32,16]{1,2,0:T(8,128)S(1)} %bitcast.149) | data formatting | bytes 524288 | tf_op jit(solution)/shard_map/transpose | solution.py:180
  52.0 4.1 %all-to-all-done.1 = f32[8,1,8192]{2,1,0:T(1,128)} async-done(((f32[8,1,8192]{2,1,0:T(1,128)}), f32[8,1,8192]{2,1,0:T(1,128)}, u32[]{:S(2)}, u32[]{:S(2)}) %all-to-all-start.1) | async-done | bytes 262176 | tf_op jit(solution)/shard_map/all_to_all | solution.py:178
  56.1 2.3 %reduce = f32[8,8192]{1,0:T(8,128)S(1)} reduce(f32[8,1,8192]{2,1,0:T(1,128)} %all-to-all-done.1, f32[]{:T(128)} %broadcast.571), dimensions={1}, to_apply=%all_to_all.43.reduce_sub_computation | reduce | bytes 524292 | tf_op jit(solution)/shard_map/all_to_all | solution.py:178
  58.3 0.3 reshape.59
  58.7 0.3 copy.135
  59.0 0.5 copy.136
  59.7 0.7 copy-done.9
  60.4 0.7 fusion.217
  61.2 0.7 fusion.222
  61.9 0.3 fusion.229
  62.2 0.6 fusion.234
  62.8 0.3 fusion.241
  63.2 0.6 fusion.246
  63.8 0.3 fusion.253
  64.1 0.6 fusion.258
  64.7 0.3 fusion.265
  65.1 0.6 fusion.270
  65.7 0.6 fusion.274
  66.3 0.5 fusion.283
  66.8 0.5 copy.137
  67.3 1.2 %reshape.60 = f32[8,1,8192]{2,1,0:T(1,128)} reshape(f32[128,16,32]{2,1,0:T(8,128)S(1)} %bitcast.146) | data formatting | bytes 524288
  68.5 3.8 %all-to-all-start.2 = ((f32[8,1,8192]{2,1,0:T(1,128)}), f32[8,1,8192]{2,1,0:T(1,128)S(1)}, u32[]{:S(2)}, u32[]{:S(2)}) async-start(f32[8,1,8192]{2,1,0:T(1,128)} %reshape.60), calls=%async_computation.2 | async-start | bytes 524288 | tf_op jit(solution)/shard_map/all_to_all | solution.py:185
  72.3 1.3 %fusion.184 = (f32[32,16,128]{2,0,1:T(8,128)}, f32[32,16,128]{2,0,1:T(8,128)S(1)}, f32[32,16,128]{2,0,1:T(8,128)S(1)}) fusion(f32[32,16,128]{2,0,1:T(8,128)S(1)} %copy-done.10, f32[32,16,128]{2,0,1:T(8,128)S(1)} %fusion.179, f32[32,16,128]{2,0,1:T(8,128)S(1)} %get-tuple-element.321, f32[32,16,128]{2,0,1:T(8,128)S(1)} %fusion.167, ...), kind=kLoop, calls=%fused_computation.376 | loop fusion | flops 917504 | bytes 2097152 | tf_op jit(solution)/shard_map/add | solution.py:74
  73.6 1.3 %fusion.200 = (f32[32,16,128]{2,0,1:T(8,128)S(1)}, f32[32,16,128]{2,0,1:T(8,128)S(1)}, f32[32,16,128]{2,0,1:T(8,128)}) fusion(f32[32,16,128]{2,0,1:T(8,128)S(1)} %get-tuple-element.318, f32[32,16,128]{2,0,1:T(8,128)S(1)} %fusion.179, f32[32,16,128]{2,0,1:T(8,128)S(1)} %get-tuple-element.319), kind=kLoop, calls=%fused_computation.392 | loop fusion | flops 786432 | bytes 1572864 | tf_op jit(solution)/shard_map/mul | solution.py:82
  74.9 6.3 %all-to-all-done.2 = f32[8,1,8192]{2,1,0:T(1,128)S(1)} async-done(((f32[8,1,8192]{2,1,0:T(1,128)}), f32[8,1,8192]{2,1,0:T(1,128)S(1)}, u32[]{:S(2)}, u32[]{:S(2)}) %all-to-all-start.2) | async-done | bytes 262176 | tf_op jit(solution)/shard_map/all_to_all | solution.py:185
  81.2 1.3 %reduce.2 = f32[8,8192]{1,0:T(8,128)S(1)} reduce(f32[8,1,8192]{2,1,0:T(1,128)S(1)} %all-to-all-done.2, f32[]{:T(128)} %broadcast.571), dimensions={1}, to_apply=%all_to_all.47.reduce_sub_computation | reduce | bytes 524292 | tf_op jit(solution)/shard_map/all_to_all | solution.py:185
  82.5 0.3 reshape.61
  83.0 0.3 copy.139
  83.3 0.6 copy-done.2
  84.3 0.5 fusion.300
  84.8 0.9 %copy.149 = f32[32,16,128]{2,1,0:T(8,128)} copy(f32[32,16,128]{2,0,1:T(8,128)S(1)} %fusion.300) | data formatting | bytes 524288 | tf_op jit(solution)/shard_map/div | solution.py:190
  (81 shorter events, 3.8 us)
Async XLA Ops:
  0.7 14.4 %collective-permute-start.1 = (f32[2,16,128]{2,1,0:T(8,128)S(1)}, f32[2,16,128]{2,1,0:T(8,128)S(1)}, u32[]{:S(2)}, u32[]{:S(2)}) collective-permute-start(f32[2,16,128]{2,1,0:T(8,128)S(1)} %get-tuple-element.418), channel_id=1, source_target_pairs={{8,0},{16,8},{24,16},{9,1},{17,9},{25,17},{10,2},{18,10},{26,18},{... | collective-permute-start | bytes 49160 | tf_op jit(solution)/shard_map/ppermute | solution.py:18
  2.0 13.1 %collective-permute-start = (f32[2,16,128]{2,1,0:T(8,128)S(1)}, f32[2,16,128]{2,1,0:T(8,128)S(1)}, u32[]{:S(2)}, u32[]{:S(2)}) collective-permute-start(f32[2,16,128]{2,1,0:T(8,128)S(1)} %get-tuple-element.417), channel_id=1, source_target_pairs={{0,8},{8,16},{16,24},{1,9},{9,17},{17,25},{2,10},{10,18},{18,26},{... | collective-permute-start | bytes 49160 | tf_op jit(solution)/shard_map/ppermute | solution.py:15
  7.7 7.4 %copy-start = (f32[32,16,128]{2,1,0:T(8,128)S(1)}, f32[32,16,128]{2,1,0:T(8,128)}, u32[]{:S(2)}) copy-start(f32[32,16,128]{2,1,0:T(8,128)} %param.5) | copy-start | bytes 786436
  7.7 33.8 %all-to-all-start = ((f32[8,1,8192]{2,1,0:T(1,128)}), f32[8,1,8192]{2,1,0:T(1,128)S(1)}, u32[]{:S(2)}, u32[]{:S(2)}) async-start(f32[8,1,8192]{2,1,0:T(1,128)} %reshape.56), calls=%async_computation | async-start | bytes 524288 | tf_op jit(solution)/shard_map/all_to_all | solution.py:177
  15.2 6.9 %collective-permute-start.2 = (f32[36,2,128]{2,0,1:T(8,128)S(1)}, f32[36,2,128]{2,0,1:T(8,128)S(1)}, u32[]{:S(2)}, u32[]{:S(2)}) collective-permute-start(f32[36,2,128]{2,0,1:T(8,128)S(1)} %copy.153), channel_id=1, source_target_pairs={{0,1},{1,2},{2,3},{3,4},{4,5},{5,6},{6,7},{8,9},{9,10},{10,11},{11... | collective-permute-start | bytes 110600 | tf_op jit(solution)/shard_map/ppermute | solution.py:15
  19.4 6.4 %collective-permute-start.3 = (f32[36,2,128]{2,0,1:T(8,128)S(1)}, f32[36,2,128]{2,0,1:T(8,128)S(1)}, u32[]{:S(2)}, u32[]{:S(2)}) collective-permute-start(f32[36,2,128]{2,0,1:T(8,128)S(1)} %copy.154), channel_id=1, source_target_pairs={{1,0},{2,1},{3,2},{4,3},{5,4},{6,5},{7,6},{9,8},{10,9},{11,10},{12... | collective-permute-start | bytes 110600 | tf_op jit(solution)/shard_map/ppermute | solution.py:18
  30.9 0.7 copy-start.1
  31.6 5.7 %copy-start.3 = (f32[32,16,128]{2,0,1:T(8,128)}, f32[32,16,128]{2,0,1:T(8,128)S(1)}, u32[]{:S(2)}) copy-start(f32[32,16,128]{2,0,1:T(8,128)S(1)} %get-tuple-element.376) | copy-start | bytes 786436
  31.6 5.7 %copy-start.5 = (f32[32,16,128]{2,0,1:T(8,128)}, f32[32,16,128]{2,0,1:T(8,128)S(1)}, u32[]{:S(2)}) copy-start(f32[32,16,128]{2,0,1:T(8,128)S(1)} %get-tuple-element.377) | copy-start | bytes 786436
  41.5 14.5 %all-to-all-start.1 = ((f32[8,1,8192]{2,1,0:T(1,128)}), f32[8,1,8192]{2,1,0:T(1,128)}, u32[]{:S(2)}, u32[]{:S(2)}) async-start(f32[8,1,8192]{2,1,0:T(1,128)} %reshape.58), calls=%async_computation.1 | async-start | bytes 524288 | tf_op jit(solution)/shard_map/all_to_all | solution.py:178
  59.5 1.0 %copy-start.9 = (f32[128,32,16]{0,2,1:T(8,128)S(1)}, f32[128,32,16]{0,2,1:T(8,128)}, u32[]{:S(2)}) copy-start(f32[128,32,16]{0,2,1:T(8,128)} %copy.132) | copy-start | bytes 786436
  68.5 3.8 %copy-start.10 = (f32[32,16,128]{2,0,1:T(8,128)S(1)}, f32[32,16,128]{2,0,1:T(8,128)}, u32[]{:S(2)}) copy-start(f32[32,16,128]{2,0,1:T(8,128)} %get-tuple-element.320) | copy-start | bytes 786436
  68.5 12.7 %all-to-all-start.2 = ((f32[8,1,8192]{2,1,0:T(1,128)}), f32[8,1,8192]{2,1,0:T(1,128)S(1)}, u32[]{:S(2)}, u32[]{:S(2)}) async-start(f32[8,1,8192]{2,1,0:T(1,128)} %reshape.60), calls=%async_computation.2 | async-start | bytes 524288 | tf_op jit(solution)/shard_map/all_to_all | solution.py:185
  83.0 1.0 %copy-start.2 = (f32[32,16,128]{2,0,1:T(8,128)S(1)}, f32[32,16,128]{2,0,1:T(8,128)}, u32[]{:S(2)}) copy-start(f32[32,16,128]{2,0,1:T(8,128)} %copy-done.1) | copy-start | bytes 786436
  83.0 1.0 %copy-start.4 = (f32[32,16,128]{2,0,1:T(8,128)S(1)}, f32[32,16,128]{2,0,1:T(8,128)}, u32[]{:S(2)}) copy-start(f32[32,16,128]{2,0,1:T(8,128)} %copy-done.3) | copy-start | bytes 786436
  83.0 1.1 %copy-start.6 = (f32[32,16,128]{2,0,1:T(8,128)S(1)}, f32[32,16,128]{2,0,1:T(8,128)}, u32[]{:S(2)}) copy-start(f32[32,16,128]{2,0,1:T(8,128)} %copy-done.5) | copy-start | bytes 786436
  83.0 1.2 %copy-start.7 = (f32[32,16,128]{2,0,1:T(8,128)S(1)}, f32[32,16,128]{2,0,1:T(8,128)}, u32[]{:S(2)}) copy-start(f32[32,16,128]{2,0,1:T(8,128)} %get-tuple-element.380) | copy-start | bytes 786436
  83.0 1.2 %copy-start.8 = (f32[32,16,128]{2,0,1:T(8,128)S(1)}, f32[32,16,128]{2,0,1:T(8,128)}, u32[]{:S(2)}) copy-start(f32[32,16,128]{2,0,1:T(8,128)} %get-tuple-element.317) | copy-start | bytes 786436
where the time goes:
time: 86.3 us; the launch traced here: 85.6 us
  starting transfers between devices  25.6 us (30%)
  other arithmetic  23.5 us (27%)
  waiting for transfers between devices  15.4 us (18%)
  local copies, waits for them, and re-layouts  14.6 us (17%)
  blocking collectives  5.61 us (7%)
    add x18, other arithmetic, cyclic_solve(): source + left_factor * shifted(source, offset, axis, 0.0)  9.81 us
    unnamed x39, local copies, waits for them, and re-layouts  8.34 us
    all_to_all x1, starting transfers between devices, shards(): lax.all_to_all(volume, 'lat', split_axis=2, concat_axis=1, tiled=True)  7.38 us
    ppermute x2, starting transfers between devices, with_halo(): lax.ppermute(lax.slice_in_dim(block, block.shape[dim] - width, None, axis...  6.95 us
    all_to_all x1, waiting for transfers between devices, shards(): lax.all_to_all(returned, 'lat', split_axis=1, concat_axis=2, tiled=True)  6.3 us
    all_gather x1, blocking collectives, shards(): gathered_z = lax.all_gather(ends_z, 'depth', axis=0, tiled=True)  5.61 us
    all_to_all x1, starting transfers between devices, shards(): lax.all_to_all(cond_y[:, 1:], 'lat', split_axis=2, concat_axis=1, tiled=T...  4.98 us
    add x10, other arithmetic, cyclic_solve(): diag = diag + left_factor * up_prev + right_factor * low_next  4.2 us
  transfers between devices with their start and end apart: 7, of which 4 were waited for; matrix products, arithmetic and copies ran while one was open for 24% of the time, Pallas kernels for 0%

commit v1 on v0

v1 whole, which is shorter than its diff:
```python
import functools

import jax
import jax.numpy as jnp
from jax import lax
from jax.experimental import pallas as pl
from jax.experimental.pallas import tpu as pltpu
from jax.sharding import PartitionSpec as P

TAU = 300.0
LAMBDA = 0.5
MESH = pl.DeviceIdType.MESH
SCALE = (64.0 * LAMBDA) ** 2
PITCH = 24
BASE = 8
LEAF = 8


def round_up(value, to):
    return (value + to - 1) // to * to


def recip(value):
    guess = pl.reciprocal(value, approx=True)
    return guess * (2.0 - value * guess)


def coupling(diff):
    return (3.0 * TAU * SCALE) * recip(SCALE + diff * diff)


def smooth_x(field):
    lane = lax.broadcasted_iota(jnp.int32, field.shape, 1)
    width = field.shape[1]
    before = jnp.where(lane == 0, 0.0, pltpu.roll(field, 1, 1))
    after = jnp.where(lane == width - 1, 0.0, pltpu.roll(field, width - 1, 1))
    return (before + after) + (field + field)


def eliminate(lo, hi, couple, source, keep):
    starts = list(range(lo, hi, LEAF))
    state = []
    for start in starts:
        state.append([1.0, couple(start - 1), source(start), None, None])
    for step in range(LEAF - 1):
        for part, start in enumerate(starts):
            excess, fill, src, excess_low, src_low = state[part]
            cell = start + step
            after = couple(cell)
            inverse = recip(excess + fill + after)
            onward = after * inverse
            back = fill * inverse
            keep(cell, onward, back, src * inverse)
            add_excess = back * excess
            add_src = back * src
            state[part] = [
                1.0 + onward * excess,
                onward * fill,
                source(cell + 1) + onward * src,
                add_excess if excess_low is None else excess_low + add_excess,
                add_src if src_low is None else src_low + add_src,
            ]
    blocks = [(start, start + LEAF, part) for start, part in zip(starts, state)]
    while len(blocks) > 1:
        merged = []
        for first, second in zip(blocks[::2], blocks[1::2]):
            e1, f1, s1, el1, sl1 = first[2]
            e2, f2, s2, el2, sl2 = second[2]
            excess = e1 + el2
            src = s1 + sl2
            inverse = recip(excess + f1 + f2)
            onward = f2 * inverse
            back = f1 * inverse
            keep(first[1] - 1, onward, back, src * inverse)
            merged.append(
                (
                    first[0],
                    second[1],
                    [
                        e2 + onward * excess,
                        onward * f1,
                        s2 + onward * src,
                        el1 + back * excess,
                        sl1 + back * src,
                    ],
                )
            )
        blocks = merged
    e, f, s, el, sl = blocks[0][2]
    return el, sl, f, e, s


def substitute(lo, hi, before, last, load, emit):
    known = {lo - 1: before, hi - 1: last}
    emit(hi - 1, last)
    size = hi - lo
    while size > LEAF:
        for start in range(lo, hi, size):
            middle = start + size // 2 - 1
            onward, back, part = load(middle)
            value = part + back * known[start - 1] + onward * known[start + size - 1]
            known[middle] = value
            emit(middle, value)
        size = size // 2
    current = {start: known[start + LEAF - 1] for start in range(lo, hi, LEAF)}
    for step in range(LEAF - 2, -1, -1):
        for start in range(lo, hi, LEAF):
            onward, back, part = load(start + step)
            value = part + back * known[start - 1] + onward * current[start]
            current[start] = value
            emit(start + step, value)


def solve_reduced(count, rows, got):
    excess = got(0, 3)
    src = got(0, 4)
    onwards, parts = [], []
    for k in range(count - 1):
        couple = got(k + 1, 2)
        excess = excess + got(k + 1, 0)
        src = src + got(k + 1, 1)
        inverse = recip(excess + couple)
        onward = couple * inverse
        onwards.append(onward)
        parts.append(src * inverse)
        excess = got(k + 1, 3) + onward * excess
        src = got(k + 1, 4) + onward * src
    value = src * recip(excess)
    values = [value]
    for k in range(count - 2, -1, -1):
        value = parts[k] + onwards[k] * value
        values.append(value)
    return values[::-1]


def kernel(
    depth_total, lat_total, planes, rows,
    vol, out,
    pack, yh, zh, cn, sm_x, sm, yy,
    zw, zv, zg, yw, yv, yg,
    zsnd, zrcv, zret, zfin, zsep, ysnd, yrcv, yret, yfin, ysep,
    halo_send, halo_recv, zs_send, zs_recv, zr_send, zr_recv,
    ys_send, ys_recv, yr_send, yr_recv,
):
    dm = lax.axis_index("depth")
    lm = lax.axis_index("lat")
    has = {
        (-1, 0): dm > 0,
        (1, 0): dm < depth_total - 1,
        (0, -1): lm > 0,
        (0, 1): lm < lat_total - 1,
    }
    for dz in (-1, 1):
        for dy in (-1, 1):
            has[(dz, dy)] = jnp.logical_and(has[(dz, 0)], has[(0, dy)])
    corners = [(dz, dy) for dz in (-1, 1) for dy in (-1, 1)]

    barrier = pltpu.get_barrier_semaphore()
    for step in range(1, lat_total):
        pl.semaphore_signal(
            barrier, inc=1, device_id=(dm, lax.rem(lm + step, lat_total)), device_id_type=MESH
        )
    for step in range(1, depth_total):
        pl.semaphore_signal(
            barrier, inc=1, device_id=(lax.rem(dm + step, depth_total), lm), device_id_type=MESH
        )
    expected = jnp.int32(lat_total + depth_total - 2)
    for dz, dy in corners:
        expected = expected + has[(dz, dy)].astype(jnp.int32)

        @pl.when(has[(dz, dy)])
        def _():
            pl.semaphore_signal(
                barrier, inc=1, device_id=(dm + dz, lm + dy), device_id_type=MESH
            )

    for side, first in ((0, 0), (1, rows - 2)):
        for j in range(2):
            pack[side, pl.ds(j, planes, stride=2), :] = vol[
                pl.ds(first + j, planes, stride=rows), :
            ]
    pl.semaphore_wait(barrier, expected)

    def halo_copy(index, way):
        dz, dy = way
        zi, yi = (dz + 1) // 2, (dy + 1) // 2
        if dy == 0:
            src = vol.at[pl.ds(0 if dz < 0 else (planes - 2) * rows, 2 * rows)]
            dst = zh.at[1 - zi]
        elif dz == 0:
            src = pack.at[yi]
            dst = yh.at[1 - yi]
        else:
            src = pack.at[yi, pl.ds(0 if dz < 0 else 2 * planes - 8, 8)]
            dst = cn.at[1 - zi, 1 - yi]
        return pltpu.make_async_remote_copy(
            src_ref=src,
            dst_ref=dst,
            send_sem=halo_send.at[index],
            recv_sem=halo_recv.at[index],
            device_id=(dm + dz, lm + dy),
            device_id_type=MESH,
        )

    ways = [(0, -1), (0, 1), (-1, 0), (1, 0)] + corners
    opposite = {way: ways.index((-way[0], -way[1])) for way in ways}
    for index, way in enumerate(ways):

        @pl.when(has[way])
        def _():
            halo_copy(index, way).start()

    def at(plane, row):
        return BASE + PITCH * (plane + 2) + row

    for plane in range(planes):
        sm_x[pl.ds(at(plane, 0), rows), :] = smooth_x(vol[pl.ds(plane * rows, rows), :])

    for index, way in enumerate(ways):
        back = opposite[way]

        @pl.when(has[way])
        def _():
            halo_copy(index, way).wait_send()
            halo_copy(back, ways[back]).wait_recv()

        @pl.when(jnp.logical_not(has[way]))
        def _():
            dz, dy = way
            zi, yi = (dz + 1) // 2, (dy + 1) // 2
            if dy == 0:
                zh[zi] = jnp.zeros(zh.shape[1:], jnp.float32)
            elif dz == 0:
                yh[yi] = jnp.zeros(yh.shape[1:], jnp.float32)
            else:
                cn[zi, yi] = jnp.zeros(cn.shape[2:], jnp.float32)

    for side, first in ((0, -2), (1, planes)):
        for j in range(2):
            sm_x[pl.ds(at(first + j, 0), rows), :] = smooth_x(zh[side, pl.ds(j * rows, rows), :])
    for side, near, edge in ((0, -1, 0), (1, rows, rows - 1)):
        far_j, near_j = (0, 1) if side == 0 else (1, 0)
        near_row = smooth_x(yh[side, pl.ds(near_j, planes, stride=2), :])
        far_row = smooth_x(yh[side, pl.ds(far_j, planes, stride=2), :])
        sm_x[pl.ds(at(0, near), planes, stride=PITCH), :] = near_row
        edge_row = sm_x[pl.ds(at(0, edge), planes, stride=PITCH), :]
        yy[side, pl.ds(8, planes), :] = (far_row + edge_row) + (near_row + near_row)
        for zside, first, base in ((0, -2, 4), (1, planes, 0)):
            tile = smooth_x(cn[zside, side])
            for j in range(2):
                k = base + 2 * j + near_j
                sm_x[pl.ds(at(first + j, near), 1), :] = tile[k : k + 1]
            j = 1 if zside == 0 else 0
            k = base + 2 * j
            near_one = tile[k + near_j : k + near_j + 1]
            far_one = tile[k + far_j : k + far_j + 1]
            edge_one = sm_x[pl.ds(at(first + j, edge), 1), :]
            yy[side, pl.ds(8 + first + j, 1), :] = (far_one + edge_one) + (near_one + near_one)

    def smooth_y(plane):
        middle = sm_x[pl.ds(at(plane, 0), rows), :]
        ends = sm_x[pl.ds(at(plane, -1), rows), :] + sm_x[pl.ds(at(plane, 1), rows), :]
        return ends + (middle + middle)

    older, old = smooth_y(-2), smooth_y(-1)
    for plane in range(-1, planes + 1):
        new = smooth_y(plane + 1)
        sm[pl.ds((plane + 1) * rows, rows), :] = (older + new) + (old + old)
        older, old = old, new

    def group_copy(axis, src, dst, send, recv, step, total, me):
        other = lax.rem(me + step, total)
        device = (other, lm) if axis == "depth" else (dm, other)
        return pltpu.make_async_remote_copy(
            src_ref=src.at[other],
            dst_ref=dst.at[me],
            send_sem=send.at[step],
            recv_sem=recv.at[total - step],
            device_id=device,
            device_id_type=MESH,
        )

    def exchange(axis, src, dst, send, recv, total, me):
        for step in range(1, total):
            group_copy(axis, src, dst, send, recv, step, total, me).start()
        dst[me] = src[me]

    def finish(axis, src, dst, send, recv, total, me):
        for step in range(1, total):
            copy = group_copy(axis, src, dst, send, recv, step, total, me)
            copy.wait_send()
            copy.wait_recv()

    def row_smoothed(row):
        if 0 <= row < rows:
            return sm[pl.ds(rows + row, planes, stride=rows), :]
        side = 0 if row < 0 else 1
        middle = yy[side, pl.ds(8, planes), :]
        ends = yy[side, pl.ds(7, planes), :] + yy[side, pl.ds(9, planes), :]
        return ends + (middle + middle)

    y_couples = {}

    def y_couple(row):
        if row not in y_couples:
            value = coupling(row_smoothed(row + 1) - row_smoothed(row))
            if row == -1:
                value = value * jnp.where(has[(0, -1)], 1.0, 0.0)
            if row == rows - 1:
                value = value * jnp.where(has[(0, 1)], 1.0, 0.0)
            y_couples[row] = value
        return y_couples[row]

    def y_keep(row, onward, back, part):
        yw[row] = onward
        yv[row] = back
        yg[row] = part

    y_chunk = planes // lat_total
    results = eliminate(
        0, rows, y_couple, lambda row: vol[pl.ds(row, planes, stride=rows), :], y_keep
    )
    for q, value in enumerate(results):
        for k in range(lat_total):
            ysnd[k, pl.ds(q * y_chunk, y_chunk), :] = value[k * y_chunk : (k + 1) * y_chunk]
    exchange("lat", ysnd, yrcv, ys_send, ys_recv, lat_total, lm)

    z_couples = {}

    def z_couple(plane):
        if plane not in z_couples:
            diff = sm[pl.ds((plane + 2) * rows, rows), :] - sm[pl.ds((plane + 1) * rows, rows), :]
            value = coupling(diff)
            if plane == -1:
                value = value * jnp.where(has[(-1, 0)], 1.0, 0.0)
            if plane == planes - 1:
                value = value * jnp.where(has[(1, 0)], 1.0, 0.0)
            z_couples[plane] = value
        return z_couples[plane]

    def z_keep(plane, onward, back, part):
        zw[plane] = onward
        zv[plane] = back
        zg[plane] = part

    z_chunk = rows // depth_total
    results = eliminate(
        0, planes, z_couple, lambda plane: vol[pl.ds(plane * rows, rows), :], z_keep
    )
    for q, value in enumerate(results):
        for k in range(depth_total):
            zsnd[k, pl.ds(q * z_chunk, z_chunk), :] = value[k * z_chunk : (k + 1) * z_chunk]
    exchange("depth", zsnd, zrcv, zs_send, zs_recv, depth_total, dm)

    group = 4 * rows

    def solve_x(step, carry):
        start = pl.multiple_of(step * group, group)
        smoothed = sm[pl.ds(rows + start, group), :]
        src = vol[pl.ds(start, group), :]
        width = src.shape[1]
        lane = lax.broadcasted_iota(jnp.int32, src.shape, 1)
        couple = jnp.where(
            lane == width - 1, 0.0, coupling(pltpu.roll(smoothed, width - 1, 1) - smoothed)
        )
        diag = 1.0 + couple + pltpu.roll(couple, 1, 1)
        offset = 1
        while offset < width:
            inverse = recip(diag)
            scaled = couple * inverse
            after = couple * pltpu.roll(inverse, width - offset, 1)
            new_diag = diag - pltpu.roll(couple * scaled, offset, 1) - couple * after
            src = (
                src
                + pltpu.roll(scaled * src, offset, 1)
                + couple * pltpu.roll(inverse * src, width - offset, 1)
            )
            if 2 * offset < width:
                couple = couple * pltpu.roll(scaled, width - offset, 1)
            diag = new_diag
            offset = offset * 2
        out[pl.ds(start, group), :] = src * recip(diag)
        return carry

    x_steps = planes * rows // group
    lax.fori_loop(0, x_steps // 2, solve_x, 0)

    def reduce_and_return(axis, snd, rcv, ret, fin, sems, total, me, chunk):
        finish(axis, snd, rcv, sems[0], sems[1], total, me)
        values = solve_reduced(
            total, chunk, lambda k, q: rcv[k, pl.ds(q * chunk, chunk), :]
        )
        for k in range(total):
            ret[k, pl.ds(0, chunk), :] = values[k - 1] if k else jnp.zeros_like(values[0])
            ret[k, pl.ds(chunk, chunk), :] = values[k]
        exchange(axis, ret, fin, sems[2], sems[3], total, me)

    y_sems = (ys_send, ys_recv, yr_send, yr_recv)
    z_sems = (zs_send, zs_recv, zr_send, zr_recv)
    reduce_and_return("lat", ysnd, yrcv, yret, yfin, y_sems, lat_total, lm, y_chunk)
    reduce_and_return("depth", zsnd, zrcv, zret, zfin, z_sems, depth_total, dm, z_chunk)
    lax.fori_loop(x_steps // 2, x_steps, solve_x, 0)

    def gather(fin, sep, total, chunk):
        for k in range(total):
            for q in range(2):
                sep[q, pl.ds(k * chunk, chunk), :] = fin[k, pl.ds(q * chunk, chunk), :]

    finish("depth", zret, zfin, zr_send, zr_recv, depth_total, dm)
    gather(zfin, zsep, depth_total, z_chunk)

    def z_emit(plane, value):
        where = pl.ds(plane * rows, rows)
        out[where, :] = out[where, :] + value

    substitute(
        0, planes, zsep[0], zsep[1], lambda p: (zw[p], zv[p], zg[p]), z_emit
    )
    finish("lat", yret, yfin, yr_send, yr_recv, lat_total, lm)
    gather(yfin, ysep, lat_total, y_chunk)

    def y_emit(row, value):
        where = pl.ds(row, planes, stride=rows)
        out[where, :] = (out[where, :] + value) * (1.0 / 3.0)

    substitute(0, rows, ysep[0], ysep[1], lambda r: (yw[r], yv[r], yg[r]), y_emit)


def shards(depth_total, lat_total, volume):
    planes, rows, columns = volume.shape
    y_chunk = planes // lat_total
    z_chunk = rows // depth_total
    f32 = jnp.float32

    def vmem(*shape):
        return pltpu.VMEM(shape + (columns,), f32)

    def dma(count):
        return pltpu.SemaphoreType.DMA((count,))

    cells = planes * rows
    out = pl.pallas_call(
        functools.partial(kernel, depth_total, lat_total, planes, rows),
        out_shape=jax.ShapeDtypeStruct((cells, columns), f32),
        in_specs=[pl.BlockSpec(memory_space=pltpu.VMEM)],
        out_specs=pl.BlockSpec(memory_space=pltpu.VMEM),
        scratch_shapes=[
            vmem(2, 2 * planes),
            vmem(2, 2 * planes),
            vmem(2, 2 * rows),
            vmem(2, 2, 8),
            vmem(BASE + PITCH * (planes + 4)),
            vmem((planes + 2) * rows),
            vmem(2, planes + 16),
            vmem(planes, rows),
            vmem(planes, rows),
            vmem(planes, rows),
            vmem(rows, planes),
            vmem(rows, planes),
            vmem(rows, planes),
            vmem(depth_total, round_up(5 * z_chunk, 8)),
            vmem(depth_total, round_up(5 * z_chunk, 8)),
            vmem(depth_total, round_up(2 * z_chunk, 8)),
            vmem(depth_total, round_up(2 * z_chunk, 8)),
            vmem(2, rows),
            vmem(lat_total, round_up(5 * y_chunk, 8)),
            vmem(lat_total, round_up(5 * y_chunk, 8)),
            vmem(lat_total, round_up(2 * y_chunk, 8)),
            vmem(lat_total, round_up(2 * y_chunk, 8)),
            vmem(2, planes),
            dma(8),
            dma(8),
            dma(depth_total),
            dma(depth_total),
            dma(depth_total),
            dma(depth_total),
            dma(lat_total),
            dma(lat_total),
            dma(lat_total),
            dma(lat_total),
        ],
        compiler_params=pltpu.CompilerParams(
            collective_id=0, has_side_effects=True, vmem_limit_bytes=24 * 1024 * 1024
        ),
        cost_estimate=pl.CostEstimate(
            flops=400 * cells * columns, bytes_accessed=8 * cells * columns, transcendentals=0
        ),
    )(volume.reshape(cells, columns))
    return out.reshape(volume.shape)


def solution(mesh):
    placed = (P("depth", "lat", None),)
    return jax.shard_map(
        functools.partial(shards, mesh.shape["depth"], mesh.shape["lat"]),
        mesh=mesh,
        in_specs=placed,
        out_specs=P("depth", "lat", None),
        check_vma=False,
    )
```

time: 86.3 us -> 21.5 us (0.25)
  starting transfers between devices: 25.6 us -> 0 us
  other arithmetic: 23.5 us -> 0 us
  Pallas kernels: 0 us -> 19.7 us
  waiting for transfers between devices: 15.4 us -> 0 us
  local copies, waits for them, and re-layouts: 14.6 us -> 1.65 us
  blocking collectives: 5.61 us -> 0 us
    pallas_call x0 -> x1, Pallas kernels: none -> 19.7 us  [shards(): pl.pallas_call(functools.partial(kernel, depth_total, lat_total, planes,...]
    all_to_all x3 -> x0, starting transfers between devices: 16.1 us -> none  [the longest x1 7.38 us: shards(): lax.all_to_all(volume, 'lat', split_axis=2, concat_axis=1, tiled=True)]
    add x28 -> x0, other arithmetic: 14 us -> none  [the longest x18 9.81 us: cyclic_solve(): source + left_factor * shifted(source, offset, axis, 0.0)]
    all_to_all x3 -> x0, waiting for transfers between devices: 10.4 us -> none  [the longest x1 6.3 us: shards(): lax.all_to_all(returned, 'lat', split_axis=1, concat_axis=2, tiled=True)]
    ppermute x4 -> x0, starting transfers between devices: 9.51 us -> none  [the longest x2 6.95 us: with_halo(): lax.ppermute(lax.slice_in_dim(block, block.shape[dim] - width, None, axis...]
    unnamed x39 -> x3, local copies, waits for them, and re-layouts: 8.34 us -> 1.65 us
    all_gather x1 -> x0, blocking collectives: 5.61 us -> none  [shards(): gathered_z = lax.all_gather(ends_z, 'depth', axis=0, tiled=True)]
    ppermute x4 -> x0, waiting for transfers between devices: 4.98 us -> none  [the longest x2 3.49 us: with_halo(): lax.ppermute(lax.slice_in_dim(block, 0, width, axis=dim), axis, backward)]
  transfers between devices with their start and end apart: 7 -> 0, of which waited for: 4 -> 0; matrix products, arithmetic and copies ran while one was open for 24% -> 0% of each run, Pallas kernels for 0% -> 0%
where the time goes in v1:
time: 21.5 us; the launch traced here: 21.4 us
  Pallas kernels  19.7 us (92%)
  local copies, waits for them, and re-layouts  1.65 us (8%)
    pallas_call x1, Pallas kernels, shards(): pl.pallas_call(functools.partial(kernel, depth_total, lat_total, planes,...  19.7 us
    unnamed x3, local copies, waits for them, and re-layouts  1.65 us

profile of v1, /device:TPU:0, one launch (start us, length us, event | category | flops | bytes accessed | tf_op | source)
XLA Modules:
  0.0 21.4 jit_solution(5639611536576129196)
XLA Ops:
  0.0 0.0 copy-start
  0.0 0.9 %copy-done = f32[32,16,128]{2,1,0:T(8,128)S(1)} copy-done((f32[32,16,128]{2,1,0:T(8,128)S(1)}, f32[32,16,128]{2,1,0:T(8,128)}, u32[]{:S(2)}) %copy-start) | copy-done | bytes 262168
  1.0 19.7 %shard_map.17 = f32[512,128]{1,0:T(8,128)S(1)} custom-call(f32[512,128]{1,0:T(8,128)S(1)} %bitcast.3), custom_call_target="tpu_custom_call" | custom-call | flops 26214400 | bytes 524288 | tf_op jit(solution)/shard_map/pallas_call | solution.py:442
  20.7 0.7 %copy.3 = f32[32,16,128]{2,1,0:T(8,128)} copy(f32[32,16,128]{2,1,0:T(8,128)S(1)} %bitcast.2) | data formatting | bytes 524288
Async XLA Ops:
  0.0 0.9 %copy-start = (f32[32,16,128]{2,1,0:T(8,128)S(1)}, f32[32,16,128]{2,1,0:T(8,128)}, u32[]{:S(2)}) copy-start(f32[32,16,128]{2,1,0:T(8,128)} %param.1) | copy-start | bytes 786436

commit v2 on v1

--- a/solution.py
+++ b/solution.py
@@ -11,8 +11,6 @@
 LAMBDA = 0.5
 MESH = pl.DeviceIdType.MESH
 SCALE = (64.0 * LAMBDA) ** 2
-PITCH = 24
-BASE = 8
 LEAF = 8
 
 
@@ -135,11 +133,11 @@
 
 def kernel(
     depth_total, lat_total, planes, rows,
-    vol, out,
-    pack, yh, zh, cn, sm_x, sm, yy,
-    zw, zv, zg, yw, yv, yg,
+    source, out,
+    vol, pack, yh, zh, cn, sm_x, sm, yy, nn,
+    vol_t, sm_t, x_out, xw, xv, xg, zw, zv, zg, yw, yv, yg,
     zsnd, zrcv, zret, zfin, zsep, ysnd, yrcv, yret, yfin, ysep,
-    halo_send, halo_recv, zs_send, zs_recv, zr_send, zr_recv,
+    load_sem, halo_send, halo_recv, zs_send, zs_recv, zr_send, zr_recv,
     ys_send, ys_recv, yr_send, yr_recv,
 ):
     dm = lax.axis_index("depth")
@@ -155,6 +153,9 @@
             has[(dz, dy)] = jnp.logical_and(has[(dz, 0)], has[(0, dy)])
     corners = [(dz, dy) for dz in (-1, 1) for dy in (-1, 1)]
 
+    load = pltpu.make_async_copy(source, vol, load_sem)
+    load.start()
+
     barrier = pltpu.get_barrier_semaphore()
     for step in range(1, lat_total):
         pl.semaphore_signal(
@@ -174,6 +175,7 @@
                 barrier, inc=1, device_id=(dm + dz, lm + dy), device_id_type=MESH
             )
 
+    load.wait()
     for side, first in ((0, 0), (1, rows - 2)):
         for j in range(2):
             pack[side, pl.ds(j, planes, stride=2), :] = vol[
@@ -210,11 +212,35 @@
         def _():
             halo_copy(index, way).start()
 
-    def at(plane, row):
-        return BASE + PITCH * (plane + 2) + row
-
-    for plane in range(planes):
-        sm_x[pl.ds(at(plane, 0), rows), :] = smooth_x(vol[pl.ds(plane * rows, rows), :])
+    def smooth_y(field):
+        row = lax.broadcasted_iota(jnp.int32, field.shape, 0)
+        before = jnp.where(row == 0, 0.0, pltpu.roll(field, 1, 0))
+        after = jnp.where(row == rows - 1, 0.0, pltpu.roll(field, rows - 1, 0))
+        return (before + after) + (field + field)
+
+    def plane_at(plane):
+        return pl.ds((plane + 1) * rows, rows)
+
+    older = old = None
+    for plane in range(planes + 1):
+        new = None
+        if plane < planes:
+            where = pl.ds(plane * rows, rows)
+            along_x = smooth_x(vol[where, :])
+            sm_x[where, :] = along_x
+            new = smooth_y(along_x)
+            if plane in (0, planes - 1):
+                sm[plane_at(-1 if plane == 0 else planes), :] = new
+        if old is not None:
+            total = old + old
+            total = total if older is None else total + older
+            sm[plane_at(plane - 1), :] = total if new is None else total + new
+        older, old = old, new
+    tile = vol.shape[1]
+    blocks = planes * rows // tile
+    for block in range(blocks):
+        where = pl.ds(block * tile, tile)
+        vol_t[where, :] = vol[where, :].T
 
     for index, way in enumerate(ways):
         back = opposite[way]
@@ -235,38 +261,38 @@
             else:
                 cn[zi, yi] = jnp.zeros(cn.shape[2:], jnp.float32)
 
-    for side, first in ((0, -2), (1, planes)):
-        for j in range(2):
-            sm_x[pl.ds(at(first + j, 0), rows), :] = smooth_x(zh[side, pl.ds(j * rows, rows), :])
-    for side, near, edge in ((0, -1, 0), (1, rows, rows - 1)):
-        far_j, near_j = (0, 1) if side == 0 else (1, 0)
+    outer_x = {}
+    for side, near, far, inner in ((0, -1, -2, 0), (1, planes, planes + 1, planes - 1)):
+        near_j, far_j = (1, 0) if side == 0 else (0, 1)
+        near_x = smooth_x(zh[side, pl.ds(near_j * rows, rows), :])
+        far_x = smooth_x(zh[side, pl.ds(far_j * rows, rows), :])
+        outer_x[side] = near_x
+        near_y = smooth_y(near_x)
+        sm[plane_at(near), :] = sm[plane_at(near), :] + smooth_y(far_x) + (near_y + near_y)
+        sm[plane_at(inner), :] = sm[plane_at(inner), :] + near_y
+    for side, edge in ((0, 0), (1, rows - 1)):
+        near_j, far_j = (1, 0) if side == 0 else (0, 1)
         near_row = smooth_x(yh[side, pl.ds(near_j, planes, stride=2), :])
         far_row = smooth_x(yh[side, pl.ds(far_j, planes, stride=2), :])
-        sm_x[pl.ds(at(0, near), planes, stride=PITCH), :] = near_row
-        edge_row = sm_x[pl.ds(at(0, edge), planes, stride=PITCH), :]
+        edge_row = sm_x[pl.ds(edge, planes, stride=rows), :]
+        nn[side, pl.ds(8, planes), :] = near_row
         yy[side, pl.ds(8, planes), :] = (far_row + edge_row) + (near_row + near_row)
-        for zside, first, base in ((0, -2, 4), (1, planes, 0)):
-            tile = smooth_x(cn[zside, side])
-            for j in range(2):
-                k = base + 2 * j + near_j
-                sm_x[pl.ds(at(first + j, near), 1), :] = tile[k : k + 1]
-            j = 1 if zside == 0 else 0
-            k = base + 2 * j
-            near_one = tile[k + near_j : k + near_j + 1]
-            far_one = tile[k + far_j : k + far_j + 1]
-            edge_one = sm_x[pl.ds(at(first + j, edge), 1), :]
-            yy[side, pl.ds(8 + first + j, 1), :] = (far_one + edge_one) + (near_one + near_one)
-
-    def smooth_y(plane):
-        middle = sm_x[pl.ds(at(plane, 0), rows), :]
-        ends = sm_x[pl.ds(at(plane, -1), rows), :] + sm_x[pl.ds(at(plane, 1), rows), :]
-        return ends + (middle + middle)
-
-    older, old = smooth_y(-2), smooth_y(-1)
-    for plane in range(-1, planes + 1):
-        new = smooth_y(plane + 1)
-        sm[pl.ds((plane + 1) * rows, rows), :] = (older + new) + (old + old)
-        older, old = old, new
+        for zside, plane, k_one, k_two in ((0, -1, 6, 4), (1, planes, 0, 2)):
+            tile_x = smooth_x(cn[zside, side])
+            near_one = tile_x[k_one + near_j : k_one + near_j + 1]
+            near_two = tile_x[k_two + near_j : k_two + near_j + 1]
+            far_one = tile_x[k_one + far_j : k_one + far_j + 1]
+            edge_one = outer_x[zside][edge : edge + 1]
+            nn[side, pl.ds(8 + plane, 1), :] = near_one
+            yy[side, pl.ds(8 + plane, 1), :] = (far_one + edge_one) + (near_one + near_one)
+            inner = 0 if zside == 0 else planes - 1
+            where = pl.ds((plane + 1) * rows + edge, 1)
+            sm[where, :] = (
+                sm[where, :] + near_row[inner : inner + 1] + near_two + (near_one + near_one)
+            )
+        where = pl.ds(rows + edge, planes, stride=rows)
+        ends = nn[side, pl.ds(7, planes), :] + nn[side, pl.ds(9, planes), :]
+        sm[where, :] = sm[where, :] + ends + (near_row + near_row)
 
     def group_copy(axis, src, dst, send, recv, step, total, me):
         other = lax.rem(me + step, total)
@@ -352,38 +378,65 @@
             zsnd[k, pl.ds(q * z_chunk, z_chunk), :] = value[k * z_chunk : (k + 1) * z_chunk]
     exchange("depth", zsnd, zrcv, zs_send, zs_recv, depth_total, dm)
 
-    group = 4 * rows
-
-    def solve_x(step, carry):
-        start = pl.multiple_of(step * group, group)
-        smoothed = sm[pl.ds(rows + start, group), :]
-        src = vol[pl.ds(start, group), :]
-        width = src.shape[1]
-        lane = lax.broadcasted_iota(jnp.int32, src.shape, 1)
-        couple = jnp.where(
-            lane == width - 1, 0.0, coupling(pltpu.roll(smoothed, width - 1, 1) - smoothed)
-        )
-        diag = 1.0 + couple + pltpu.roll(couple, 1, 1)
-        offset = 1
-        while offset < width:
-            inverse = recip(diag)
-            scaled = couple * inverse
-            after = couple * pltpu.roll(inverse, width - offset, 1)
-            new_diag = diag - pltpu.roll(couple * scaled, offset, 1) - couple * after
-            src = (
-                src
-                + pltpu.roll(scaled * src, offset, 1)
-                + couple * pltpu.roll(inverse * src, width - offset, 1)
-            )
-            if 2 * offset < width:
-                couple = couple * pltpu.roll(scaled, width - offset, 1)
-            diag = new_diag
-            offset = offset * 2
-        out[pl.ds(start, group), :] = src * recip(diag)
-        return carry
-
-    x_steps = planes * rows // group
-    lax.fori_loop(0, x_steps // 2, solve_x, 0)
+    for block in range(blocks):
+        where = pl.ds(block * tile, tile)
+        sm_t[where, :] = sm[pl.ds(rows + block * tile, tile), :].T
+    cells = tile // 8
+    spread = blocks * 8
+
+    def x_at(cell):
+        return pl.ds(cell, spread, stride=cells)
+
+    def turn(field, by):
+        return pltpu.roll(field.reshape(blocks, 8, tile), by, 1).reshape(spread, tile)
+
+    x_couples = {}
+
+    def x_couple(cell):
+        if cell not in x_couples:
+            if cell == -1:
+                value = turn(x_couple(cells - 1), 1)
+            elif cell == cells - 1:
+                sub = lax.rem(lax.broadcasted_iota(jnp.int32, (spread, tile), 0), 8)
+                diff = turn(sm_t[x_at(0), :], 7) - sm_t[x_at(cell), :]
+                value = jnp.where(sub == 7, 0.0, coupling(diff))
+            else:
+                value = coupling(sm_t[x_at(cell + 1), :] - sm_t[x_at(cell), :])
+            x_couples[cell] = value
+        return x_couples[cell]
+
+    def x_keep(cell, onward, back, part):
+        xw[cell] = onward
+        xv[cell] = back
+        xg[cell] = part
+
+    excess_low, src_low, couple, excess, src = eliminate(
+        0, cells, x_couple, lambda cell: vol_t[x_at(cell), :], x_keep
+    )
+    diag = excess + turn(excess_low, 7) + couple
+    src = src + turn(src_low, 7)
+    couple = turn(couple, 7)
+    diag = diag + couple
+    offset = 1
+    while offset < 8:
+        inverse = recip(diag)
+        scaled = couple * inverse
+        after = couple * turn(inverse, 8 - offset)
+        new_diag = diag - turn(couple * scaled, offset) - couple * after
+        src = src + turn(scaled * src, offset) + couple * turn(inverse * src, 8 - offset)
+        if 2 * offset < 8:
+            couple = couple * turn(scaled, 8 - offset)
+        diag = new_diag
+        offset = offset * 2
+    last = src * recip(diag)
+
+    def x_emit(cell, value):
+        x_out[x_at(cell), :] = value
+
+    substitute(0, cells, turn(last, 1), last, lambda c: (xw[c], xv[c], xg[c]), x_emit)
+    for block in range(blocks):
+        where = pl.ds(block * tile, tile)
+        out[where, :] = x_out[where, :].T
 
     def reduce_and_return(axis, snd, rcv, ret, fin, sems, total, me, chunk):
         finish(axis, snd, rcv, sems[0], sems[1], total, me)
@@ -399,7 +452,6 @@
     z_sems = (zs_send, zs_recv, zr_send, zr_recv)
     reduce_and_return("lat", ysnd, yrcv, yret, yfin, y_sems, lat_total, lm, y_chunk)
     reduce_and_return("depth", zsnd, zrcv, zret, zfin, z_sems, depth_total, dm, z_chunk)
-    lax.fori_loop(x_steps // 2, x_steps, solve_x, 0)
 
     def gather(fin, sep, total, chunk):
         for k in range(total):
@@ -442,16 +494,24 @@
     out = pl.pallas_call(
         functools.partial(kernel, depth_total, lat_total, planes, rows),
         out_shape=jax.ShapeDtypeStruct((cells, columns), f32),
-        in_specs=[pl.BlockSpec(memory_space=pltpu.VMEM)],
+        in_specs=[pl.BlockSpec(memory_space=pltpu.HBM)],
         out_specs=pl.BlockSpec(memory_space=pltpu.VMEM),
         scratch_shapes=[
+            vmem(cells),
             vmem(2, 2 * planes),
             vmem(2, 2 * planes),
             vmem(2, 2 * rows),
             vmem(2, 2, 8),
-            vmem(BASE + PITCH * (planes + 4)),
+            vmem(cells),
             vmem((planes + 2) * rows),
             vmem(2, planes + 16),
+            vmem(2, planes + 16),
+            vmem(cells),
+            vmem(cells),
+            vmem(cells),
+            vmem(columns // 8, cells * 8 // columns),
+            vmem(columns // 8, cells * 8 // columns),
+            vmem(columns // 8, cells * 8 // columns),
             vmem(planes, rows),
             vmem(planes, rows),
             vmem(planes, rows),
@@ -468,6 +528,7 @@
             vmem(lat_total, round_up(2 * y_chunk, 8)),
             vmem(lat_total, round_up(2 * y_chunk, 8)),
             vmem(2, planes),
+            pltpu.SemaphoreType.DMA,
             dma(8),
             dma(8),
             dma(depth_total),

time: 21.5 us -> 21.5 us (level)
  no operation moved by 1% of the time
where the time goes in v2:
time: 21.5 us; the launch traced here: 21.3 us
  Pallas kernels  19.7 us (92%)
  local copies, waits for them, and re-layouts  1.65 us (8%)
    pallas_call x1, Pallas kernels, shards(): pl.pallas_call(functools.partial(kernel, depth_total, lat_total, planes,...  19.7 us
    unnamed x3, local copies, waits for them, and re-layouts  1.65 us

profile of v2, /device:TPU:0, one launch (start us, length us, event | category | flops | bytes accessed | tf_op | source)
XLA Modules:
  0.0 21.3 jit_solution(17722132648697499661)
XLA Ops:
  0.0 0.0 copy-start
  0.0 0.9 %copy-done = f32[32,16,128]{2,1,0:T(8,128)S(1)} copy-done((f32[32,16,128]{2,1,0:T(8,128)S(1)}, f32[32,16,128]{2,1,0:T(8,128)}, u32[]{:S(2)}) %copy-start) | copy-done | bytes 262168
  1.0 19.7 %shard_map.17 = f32[512,128]{1,0:T(8,128)S(1)} custom-call(f32[512,128]{1,0:T(8,128)S(1)} %bitcast.3), custom_call_target="tpu_custom_call" | custom-call | flops 26214400 | bytes 524288 | tf_op jit(solution)/shard_map/pallas_call | solution.py:494
  20.6 0.7 %copy.3 = f32[32,16,128]{2,1,0:T(8,128)} copy(f32[32,16,128]{2,1,0:T(8,128)S(1)} %bitcast.2) | data formatting | bytes 524288
Async XLA Ops:
  0.0 0.9 %copy-start = (f32[32,16,128]{2,1,0:T(8,128)S(1)}, f32[32,16,128]{2,1,0:T(8,128)}, u32[]{:S(2)}) copy-start(f32[32,16,128]{2,1,0:T(8,128)} %param.1) | copy-start | bytes 786436

commit v3 on v2

--- a/solution.py
+++ b/solution.py
@@ -12,10 +12,6 @@
 MESH = pl.DeviceIdType.MESH
 SCALE = (64.0 * LAMBDA) ** 2
 LEAF = 8
-
-
-def round_up(value, to):
-    return (value + to - 1) // to * to
 
 
 def recip(value):
@@ -247,7 +243,6 @@
 
         @pl.when(has[way])
         def _():
-            halo_copy(index, way).wait_send()
             halo_copy(back, ways[back]).wait_recv()
 
         @pl.when(jnp.logical_not(has[way]))
@@ -294,28 +289,22 @@
         ends = nn[side, pl.ds(7, planes), :] + nn[side, pl.ds(9, planes), :]
         sm[where, :] = sm[where, :] + ends + (near_row + near_row)
 
-    def group_copy(axis, src, dst, send, recv, step, total, me):
-        other = lax.rem(me + step, total)
-        device = (other, lm) if axis == "depth" else (dm, other)
-        return pltpu.make_async_remote_copy(
-            src_ref=src.at[other],
-            dst_ref=dst.at[me],
-            send_sem=send.at[step],
-            recv_sem=recv.at[total - step],
-            device_id=device,
-            device_id_type=MESH,
-        )
-
-    def exchange(axis, src, dst, send, recv, total, me):
+    def exchange(axis, src, dst, sems, total, me):
         for step in range(1, total):
-            group_copy(axis, src, dst, send, recv, step, total, me).start()
+            other = lax.rem(me + step, total)
+            pltpu.make_async_remote_copy(
+                src_ref=src.at[other],
+                dst_ref=dst.at[me],
+                send_sem=sems[0],
+                recv_sem=sems[1],
+                device_id=(other, lm) if axis == "depth" else (dm, other),
+                device_id_type=MESH,
+            ).start()
         dst[me] = src[me]
 
-    def finish(axis, src, dst, send, recv, total, me):
-        for step in range(1, total):
-            copy = group_copy(axis, src, dst, send, recv, step, total, me)
-            copy.wait_send()
-            copy.wait_recv()
+    def wait_all(ref, sem, total):
+        some = ref.at[pl.ds(0, total - 1)]
+        pltpu.make_async_copy(some, some, sem).wait()
 
     def row_smoothed(row):
         if 0 <= row < rows:
@@ -349,7 +338,7 @@
     for q, value in enumerate(results):
         for k in range(lat_total):
             ysnd[k, pl.ds(q * y_chunk, y_chunk), :] = value[k * y_chunk : (k + 1) * y_chunk]
-    exchange("lat", ysnd, yrcv, ys_send, ys_recv, lat_total, lm)
+    exchange("lat", ysnd, yrcv, (ys_send, ys_recv), lat_total, lm)
 
     z_couples = {}
 
@@ -376,7 +365,7 @@
     for q, value in enumerate(results):
         for k in range(depth_total):
             zsnd[k, pl.ds(q * z_chunk, z_chunk), :] = value[k * z_chunk : (k + 1) * z_chunk]
-    exchange("depth", zsnd, zrcv, zs_send, zs_recv, depth_total, dm)
+    exchange("depth", zsnd, zrcv, (zs_send, zs_recv), depth_total, dm)
 
     for block in range(blocks):
         where = pl.ds(block * tile, tile)
@@ -438,27 +427,27 @@
         where = pl.ds(block * tile, tile)
         out[where, :] = x_out[where, :].T
 
-    def reduce_and_return(axis, snd, rcv, ret, fin, sems, total, me, chunk):
-        finish(axis, snd, rcv, sems[0], sems[1], total, me)
+    def reduce_and_return(axis, rcv, ret, fin, recv, sems, total, me, chunk):
+        wait_all(rcv, recv, total)
         values = solve_reduced(
             total, chunk, lambda k, q: rcv[k, pl.ds(q * chunk, chunk), :]
         )
         for k in range(total):
             ret[k, pl.ds(0, chunk), :] = values[k - 1] if k else jnp.zeros_like(values[0])
             ret[k, pl.ds(chunk, chunk), :] = values[k]
-        exchange(axis, ret, fin, sems[2], sems[3], total, me)
-
-    y_sems = (ys_send, ys_recv, yr_send, yr_recv)
-    z_sems = (zs_send, zs_recv, zr_send, zr_recv)
-    reduce_and_return("lat", ysnd, yrcv, yret, yfin, y_sems, lat_total, lm, y_chunk)
-    reduce_and_return("depth", zsnd, zrcv, zret, zfin, z_sems, depth_total, dm, z_chunk)
+        exchange(axis, ret, fin, sems, total, me)
+
+    y_sems = (yr_send, yr_recv)
+    z_sems = (zr_send, zr_recv)
+    reduce_and_return("lat", yrcv, yret, yfin, ys_recv, y_sems, lat_total, lm, y_chunk)
+    reduce_and_return("depth", zrcv, zret, zfin, zs_recv, z_sems, depth_total, dm, z_chunk)
 
     def gather(fin, sep, total, chunk):
         for k in range(total):
             for q in range(2):
                 sep[q, pl.ds(k * chunk, chunk), :] = fin[k, pl.ds(q * chunk, chunk), :]
 
-    finish("depth", zret, zfin, zr_send, zr_recv, depth_total, dm)
+    wait_all(zfin, zr_recv, depth_total)
     gather(zfin, zsep, depth_total, z_chunk)
 
     def z_emit(plane, value):
@@ -468,7 +457,7 @@
     substitute(
         0, planes, zsep[0], zsep[1], lambda p: (zw[p], zv[p], zg[p]), z_emit
     )
-    finish("lat", yret, yfin, yr_send, yr_recv, lat_total, lm)
+    wait_all(yfin, yr_recv, lat_total)
     gather(yfin, ysep, lat_total, y_chunk)
 
     def y_emit(row, value):
@@ -476,6 +465,18 @@
         out[where, :] = (out[where, :] + value) * (1.0 / 3.0)
 
     substitute(0, rows, ysep[0], ysep[1], lambda r: (yw[r], yv[r], yg[r]), y_emit)
+    for ref, sem, total in (
+        (ysnd, ys_send, lat_total),
+        (yret, yr_send, lat_total),
+        (zsnd, zs_send, depth_total),
+        (zret, zr_send, depth_total),
+    ):
+        wait_all(ref, sem, total)
+    for index, way in enumerate(ways):
+
+        @pl.when(has[way])
+        def _():
+            halo_copy(index, way).wait_send()
 
 
 def shards(depth_total, lat_total, volume):
@@ -518,27 +519,27 @@
             vmem(rows, planes),
             vmem(rows, planes),
             vmem(rows, planes),
-            vmem(depth_total, round_up(5 * z_chunk, 8)),
-            vmem(depth_total, round_up(5 * z_chunk, 8)),
-            vmem(depth_total, round_up(2 * z_chunk, 8)),
-            vmem(depth_total, round_up(2 * z_chunk, 8)),
+            vmem(depth_total, 5 * z_chunk),
+            vmem(depth_total, 5 * z_chunk),
+            vmem(depth_total, 2 * z_chunk),
+            vmem(depth_total, 2 * z_chunk),
             vmem(2, rows),
-            vmem(lat_total, round_up(5 * y_chunk, 8)),
-            vmem(lat_total, round_up(5 * y_chunk, 8)),
-            vmem(lat_total, round_up(2 * y_chunk, 8)),
-            vmem(lat_total, round_up(2 * y_chunk, 8)),
+            vmem(lat_total, 5 * y_chunk),
+            vmem(lat_total, 5 * y_chunk),
+            vmem(lat_total, 2 * y_chunk),
+            vmem(lat_total, 2 * y_chunk),
             vmem(2, planes),
             pltpu.SemaphoreType.DMA,
             dma(8),
             dma(8),
-            dma(depth_total),
-            dma(depth_total),
-            dma(depth_total),
-            dma(depth_total),
-            dma(lat_total),
-            dma(lat_total),
-            dma(lat_total),
-            dma(lat_total),
+            pltpu.SemaphoreType.DMA,
+            pltpu.SemaphoreType.DMA,
+            pltpu.SemaphoreType.DMA,
+            pltpu.SemaphoreType.DMA,
+            pltpu.SemaphoreType.DMA,
+            pltpu.SemaphoreType.DMA,
+            pltpu.SemaphoreType.DMA,
+            pltpu.SemaphoreType.DMA,
         ],
         compiler_params=pltpu.CompilerParams(
             collective_id=0, has_side_effects=True, vmem_limit_bytes=24 * 1024 * 1024
@@ -546,7 +547,7 @@
         cost_estimate=pl.CostEstimate(
             flops=400 * cells * columns, bytes_accessed=8 * cells * columns, transcendentals=0
         ),
-    )(volume.reshape(cells, columns))
+    )(pltpu.with_memory_space_constraint(volume.reshape(cells, columns), pltpu.HBM))
     return out.reshape(volume.shape)
 
 

time: 21.5 us -> 19.8 us (0.921)
  local copies, waits for them, and re-layouts: 1.65 us -> 0.71 us
  Pallas kernels: 19.7 us -> 18.9 us
    unnamed x3 -> x1, local copies, waits for them, and re-layouts: 1.65 us -> 0.71 us
    pallas_call x1, Pallas kernels: 19.7 us -> 18.9 us  [shards(): pl.pallas_call(functools.partial(kernel, depth_total, lat_total, planes,...]
where the time goes in v3:
time: 19.8 us; the launch traced here: 19.6 us
  Pallas kernels  18.9 us (95%)
  local copies, waits for them, and re-layouts  0.71 us (4%)
    pallas_call x1, Pallas kernels, shards(): pl.pallas_call(functools.partial(kernel, depth_total, lat_total, planes,...  18.9 us
    unnamed x1, local copies, waits for them, and re-layouts  0.71 us

profile of v3, /device:TPU:0, one launch (start us, length us, event | category | flops | bytes accessed | tf_op | source)
XLA Modules:
  0.0 19.6 jit_solution(3494528289072773099)
XLA Ops:
  0.0 18.9 %shard_map.17 = f32[512,128]{1,0:T(8,128)S(1)} custom-call(f32[512,128]{1,0:T(8,128)} %bitcast.3), custom_call_target="tpu_custom_call" | custom-call | flops 26214400 | bytes 524288 | tf_op jit(solution)/shard_map/pallas_call | solution.py:495
  18.9 0.7 %copy.3 = f32[32,16,128]{2,1,0:T(8,128)} copy(f32[32,16,128]{2,1,0:T(8,128)S(1)} %bitcast.2) | data formatting | bytes 524288

commit v4 on v3

--- a/solution.py
+++ b/solution.py
@@ -130,7 +130,7 @@
 def kernel(
     depth_total, lat_total, planes, rows,
     source, out,
-    vol, pack, yh, zh, cn, sm_x, sm, yy, nn,
+    vol, pack_one, pack_two, yh_one, yh_two, zh_one, zh_two, cn, sm_x, sm, yy, nn,
     vol_t, sm_t, x_out, xw, xv, xg, zw, zv, zg, yw, yv, yg,
     zsnd, zrcv, zret, zfin, zsep, ysnd, yrcv, yret, yfin, ysep,
     load_sem, halo_send, halo_recv, zs_send, zs_recv, zr_send, zr_recv,
@@ -172,24 +172,22 @@
             )
 
     load.wait()
-    for side, first in ((0, 0), (1, rows - 2)):
-        for j in range(2):
-            pack[side, pl.ds(j, planes, stride=2), :] = vol[
-                pl.ds(first + j, planes, stride=rows), :
-            ]
+    pack_one[...] = vol[pl.ds(0, planes, stride=rows), :]
+    for j in range(2):
+        pack_two[pl.ds(j, planes, stride=2), :] = vol[pl.ds(rows - 2 + j, planes, stride=rows), :]
     pl.semaphore_wait(barrier, expected)
 
     def halo_copy(index, way):
         dz, dy = way
         zi, yi = (dz + 1) // 2, (dy + 1) // 2
         if dy == 0:
-            src = vol.at[pl.ds(0 if dz < 0 else (planes - 2) * rows, 2 * rows)]
-            dst = zh.at[1 - zi]
+            src = vol.at[pl.ds(0, rows) if dz < 0 else pl.ds((planes - 2) * rows, 2 * rows)]
+            dst = zh_one if dz < 0 else zh_two
         elif dz == 0:
-            src = pack.at[yi]
-            dst = yh.at[1 - yi]
+            src, dst = (pack_one, yh_one) if dy < 0 else (pack_two, yh_two)
         else:
-            src = pack.at[yi, pl.ds(0 if dz < 0 else 2 * planes - 8, 8)]
+            pack, count = (pack_one, planes) if dy < 0 else (pack_two, 2 * planes)
+            src = pack.at[pl.ds(0 if dz < 0 else count - 8, 8)]
             dst = cn.at[1 - zi, 1 - yi]
         return pltpu.make_async_remote_copy(
             src_ref=src,
@@ -225,8 +223,8 @@
             along_x = smooth_x(vol[where, :])
             sm_x[where, :] = along_x
             new = smooth_y(along_x)
-            if plane in (0, planes - 1):
-                sm[plane_at(-1 if plane == 0 else planes), :] = new
+            if plane == 0:
+                sm[plane_at(-1), :] = new
         if old is not None:
             total = old + old
             total = total if older is None else total + older
@@ -250,47 +248,49 @@
             dz, dy = way
             zi, yi = (dz + 1) // 2, (dy + 1) // 2
             if dy == 0:
-                zh[zi] = jnp.zeros(zh.shape[1:], jnp.float32)
+                ref = zh_two if dz < 0 else zh_one
+                ref[...] = jnp.zeros(ref.shape, jnp.float32)
             elif dz == 0:
-                yh[yi] = jnp.zeros(yh.shape[1:], jnp.float32)
+                ref = yh_two if dy < 0 else yh_one
+                ref[...] = jnp.zeros(ref.shape, jnp.float32)
             else:
                 cn[zi, yi] = jnp.zeros(cn.shape[2:], jnp.float32)
 
-    outer_x = {}
-    for side, near, far, inner in ((0, -1, -2, 0), (1, planes, planes + 1, planes - 1)):
-        near_j, far_j = (1, 0) if side == 0 else (0, 1)
-        near_x = smooth_x(zh[side, pl.ds(near_j * rows, rows), :])
-        far_x = smooth_x(zh[side, pl.ds(far_j * rows, rows), :])
-        outer_x[side] = near_x
-        near_y = smooth_y(near_x)
-        sm[plane_at(near), :] = sm[plane_at(near), :] + smooth_y(far_x) + (near_y + near_y)
-        sm[plane_at(inner), :] = sm[plane_at(inner), :] + near_y
-    for side, edge in ((0, 0), (1, rows - 1)):
-        near_j, far_j = (1, 0) if side == 0 else (0, 1)
-        near_row = smooth_x(yh[side, pl.ds(near_j, planes, stride=2), :])
-        far_row = smooth_x(yh[side, pl.ds(far_j, planes, stride=2), :])
-        edge_row = sm_x[pl.ds(edge, planes, stride=rows), :]
-        nn[side, pl.ds(8, planes), :] = near_row
-        yy[side, pl.ds(8, planes), :] = (far_row + edge_row) + (near_row + near_row)
-        for zside, plane, k_one, k_two in ((0, -1, 6, 4), (1, planes, 0, 2)):
-            tile_x = smooth_x(cn[zside, side])
-            near_one = tile_x[k_one + near_j : k_one + near_j + 1]
-            near_two = tile_x[k_two + near_j : k_two + near_j + 1]
-            far_one = tile_x[k_one + far_j : k_one + far_j + 1]
-            edge_one = outer_x[zside][edge : edge + 1]
-            nn[side, pl.ds(8 + plane, 1), :] = near_one
-            yy[side, pl.ds(8 + plane, 1), :] = (far_one + edge_one) + (near_one + near_one)
-            inner = 0 if zside == 0 else planes - 1
-            where = pl.ds((plane + 1) * rows + edge, 1)
-            sm[where, :] = (
-                sm[where, :] + near_row[inner : inner + 1] + near_two + (near_one + near_one)
-            )
+    far_x = smooth_x(zh_two[pl.ds(0, rows), :])
+    low_x = smooth_x(zh_two[pl.ds(rows, rows), :])
+    high_x = smooth_x(zh_one[...])
+    low_y = smooth_y(low_x)
+    sm[plane_at(-1), :] = sm[plane_at(-1), :] + smooth_y(far_x) + (low_y + low_y)
+    sm[plane_at(0), :] = sm[plane_at(0), :] + low_y
+    sm[plane_at(planes - 1), :] = sm[plane_at(planes - 1), :] + smooth_y(high_x)
+    low_tile = smooth_x(cn[0, 0])
+    high_tile = smooth_x(cn[1, 0])
+    far_row = smooth_x(yh_two[pl.ds(0, planes, stride=2), :])
+    low_row = smooth_x(yh_two[pl.ds(1, planes, stride=2), :])
+    edge_row = sm_x[pl.ds(0, planes, stride=rows), :]
+    yy[pl.ds(8, planes), :] = (far_row + edge_row) + (low_row + low_row)
+    for where, plane_x, far_one, near_one in (
+        (7, low_x, low_tile[6:7], low_tile[7:8]),
+        (8 + planes, high_x, high_tile[0:1], high_tile[1:2]),
+    ):
+        yy[pl.ds(where, 1), :] = (far_one + plane_x[0:1]) + (near_one + near_one)
+    low_side = (0, 0, low_row, low_tile[5:6], low_tile[7:8], high_tile[1:2])
+    low_tile = smooth_x(cn[0, 1])
+    high_tile = smooth_x(cn[1, 1])
+    high_row = smooth_x(yh_one[...])
+    high_side = (1, rows - 1, high_row, low_tile[6:7], low_tile[7:8], high_tile[0:1])
+    for side, edge, row, two_before, before, after in (low_side, high_side):
+        where = pl.ds(edge, 1)
+        sm[where, :] = sm[where, :] + row[0:1] + two_before + (before + before)
+        nn[side, pl.ds(8, planes), :] = row
+        nn[side, pl.ds(7, 1), :] = before
+        nn[side, pl.ds(8 + planes, 1), :] = after
         where = pl.ds(rows + edge, planes, stride=rows)
         ends = nn[side, pl.ds(7, planes), :] + nn[side, pl.ds(9, planes), :]
-        sm[where, :] = sm[where, :] + ends + (near_row + near_row)
+        sm[where, :] = sm[where, :] + ends + (row + row)
 
     def exchange(axis, src, dst, sems, total, me):
-        for step in range(1, total):
+        for step in sorted(range(1, total), key=lambda step: abs(2 * step - total)):
             other = lax.rem(me + step, total)
             pltpu.make_async_remote_copy(
                 src_ref=src.at[other],
@@ -309,9 +309,8 @@
     def row_smoothed(row):
         if 0 <= row < rows:
             return sm[pl.ds(rows + row, planes, stride=rows), :]
-        side = 0 if row < 0 else 1
-        middle = yy[side, pl.ds(8, planes), :]
-        ends = yy[side, pl.ds(7, planes), :] + yy[side, pl.ds(9, planes), :]
+        middle = yy[pl.ds(8, planes), :]
+        ends = yy[pl.ds(7, planes), :] + yy[pl.ds(9, planes), :]
         return ends + (middle + middle)
 
     y_couples = {}
@@ -321,8 +320,6 @@
             value = coupling(row_smoothed(row + 1) - row_smoothed(row))
             if row == -1:
                 value = value * jnp.where(has[(0, -1)], 1.0, 0.0)
-            if row == rows - 1:
-                value = value * jnp.where(has[(0, 1)], 1.0, 0.0)
             y_couples[row] = value
         return y_couples[row]
 
@@ -348,8 +345,6 @@
             value = coupling(diff)
             if plane == -1:
                 value = value * jnp.where(has[(-1, 0)], 1.0, 0.0)
-            if plane == planes - 1:
-                value = value * jnp.where(has[(1, 0)], 1.0, 0.0)
             z_couples[plane] = value
         return z_couples[plane]
 
@@ -499,13 +494,16 @@
         out_specs=pl.BlockSpec(memory_space=pltpu.VMEM),
         scratch_shapes=[
             vmem(cells),
-            vmem(2, 2 * planes),
-            vmem(2, 2 * planes),
-            vmem(2, 2 * rows),
+            vmem(planes),
+            vmem(2 * planes),
+            vmem(planes),
+            vmem(2 * planes),
+            vmem(rows),
+            vmem(2 * rows),
             vmem(2, 2, 8),
             vmem(cells),
-            vmem((planes + 2) * rows),
-            vmem(2, planes + 16),
+            vmem((planes + 1) * rows),
+            vmem(planes + 16),
             vmem(2, planes + 16),
             vmem(cells),
             vmem(cells),

time: 19.8 us -> 19.7 us (level)
  no operation moved by 1% of the time
where the time goes in v4:
time: 19.7 us; the launch traced here: 19.6 us
  Pallas kernels  18.8 us (95%)
  local copies, waits for them, and re-layouts  0.71 us (4%)
    pallas_call x1, Pallas kernels, shards(): pl.pallas_call(functools.partial(kernel, depth_total, lat_total, planes,...  18.8 us
    unnamed x1, local copies, waits for them, and re-layouts  0.71 us

profile of v4, /device:TPU:0, one launch (start us, length us, event | category | flops | bytes accessed | tf_op | source)
XLA Modules:
  0.0 19.6 jit_solution(5307207827084110595)
XLA Ops:
  0.0 18.8 %shard_map.17 = f32[512,128]{1,0:T(8,128)S(1)} custom-call(f32[512,128]{1,0:T(8,128)} %bitcast.3), custom_call_target="tpu_custom_call" | custom-call | flops 26214400 | bytes 524288 | tf_op jit(solution)/shard_map/pallas_call | solution.py:490
  18.8 0.7 %copy.3 = f32[32,16,128]{2,1,0:T(8,128)} copy(f32[32,16,128]{2,1,0:T(8,128)S(1)} %bitcast.2) | data formatting | bytes 524288

commit v5 on v4

--- a/solution.py
+++ b/solution.py
@@ -33,27 +33,34 @@
 
 def eliminate(lo, hi, couple, source, keep):
     starts = list(range(lo, hi, LEAF))
-    state = []
+    init = []
     for start in starts:
-        state.append([1.0, couple(start - 1), source(start), None, None])
-    for step in range(LEAF - 1):
-        for part, start in enumerate(starts):
-            excess, fill, src, excess_low, src_low = state[part]
+        src = source(start)
+        zero = jnp.zeros_like(src)
+        init.append((zero + 1.0, couple(start - 1), src, zero, zero, couple(start)))
+
+    def body(step, carry):
+        state = []
+        for start, (excess, fill, src, excess_low, src_low, after) in zip(starts, carry):
             cell = start + step
-            after = couple(cell)
             inverse = recip(excess + fill + after)
             onward = after * inverse
             back = fill * inverse
             keep(cell, onward, back, src * inverse)
-            add_excess = back * excess
-            add_src = back * src
-            state[part] = [
-                1.0 + onward * excess,
-                onward * fill,
-                source(cell + 1) + onward * src,
-                add_excess if excess_low is None else excess_low + add_excess,
-                add_src if src_low is None else src_low + add_src,
-            ]
+            state.append(
+                (
+                    1.0 + onward * excess,
+                    onward * fill,
+                    source(cell + 1) + onward * src,
+                    excess_low + back * excess,
+                    src_low + back * src,
+                    couple(cell + 1),
+                )
+            )
+        return tuple(state)
+
+    state = lax.fori_loop(0, LEAF - 1, body, tuple(init))
+    state = [part[:5] for part in state]
     blocks = [(start, start + LEAF, part) for start, part in zip(starts, state)]
     while len(blocks) > 1:
         merged = []
@@ -96,13 +103,19 @@
             known[middle] = value
             emit(middle, value)
         size = size // 2
-    current = {start: known[start + LEAF - 1] for start in range(lo, hi, LEAF)}
-    for step in range(LEAF - 2, -1, -1):
-        for start in range(lo, hi, LEAF):
-            onward, back, part = load(start + step)
-            value = part + back * known[start - 1] + onward * current[start]
-            current[start] = value
-            emit(start + step, value)
+    starts = list(range(lo, hi, LEAF))
+
+    def body(step, carry):
+        current = []
+        for start, later in zip(starts, carry):
+            cell = start + (LEAF - 2) - step
+            onward, back, part = load(cell)
+            value = part + back * known[start - 1] + onward * later
+            current.append(value)
+            emit(cell, value)
+        return tuple(current)
+
+    lax.fori_loop(0, LEAF - 1, body, tuple(known[start + LEAF - 1] for start in starts))
 
 
 def solve_reduced(count, rows, got):
@@ -215,26 +228,34 @@
     def plane_at(plane):
         return pl.ds((plane + 1) * rows, rows)
 
-    older = old = None
-    for plane in range(planes + 1):
-        new = None
-        if plane < planes:
-            where = pl.ds(plane * rows, rows)
-            along_x = smooth_x(vol[where, :])
-            sm_x[where, :] = along_x
+    group = 4
+
+    def smooth_planes(step, carry):
+        older, old = carry
+        for plane in range(group):
+            start = pl.multiple_of((step * group + plane) * rows, rows)
+            along_x = smooth_x(vol[pl.ds(start, rows), :])
+            sm_x[pl.ds(start, rows), :] = along_x
             new = smooth_y(along_x)
-            if plane == 0:
-                sm[plane_at(-1), :] = new
-        if old is not None:
-            total = old + old
-            total = total if older is None else total + older
-            sm[plane_at(plane - 1), :] = total if new is None else total + new
-        older, old = old, new
+            sm[pl.ds(start, rows), :] = (older + new) + (old + old)
+            older, old = old, new
+        return older, old
+
+    zero = jnp.zeros((rows, vol.shape[1]), jnp.float32)
+    older, old = lax.fori_loop(0, planes // group, smooth_planes, (zero, zero))
+    sm[plane_at(planes - 1), :] = older + (old + old)
     tile = vol.shape[1]
     blocks = planes * rows // tile
-    for block in range(blocks):
-        where = pl.ds(block * tile, tile)
-        vol_t[where, :] = vol[where, :].T
+
+    def turn_tiles(src, shift, dst):
+        def body(block, carry):
+            start = pl.multiple_of(block * tile, tile)
+            dst[pl.ds(start, tile), :] = src[pl.ds(shift + start, tile), :].T
+            return carry
+
+        lax.fori_loop(0, blocks, body, 0)
+
+    turn_tiles(vol, 0, vol_t)
 
     for index, way in enumerate(ways):
         back = opposite[way]
@@ -307,21 +328,15 @@
         pltpu.make_async_copy(some, some, sem).wait()
 
     def row_smoothed(row):
-        if 0 <= row < rows:
-            return sm[pl.ds(rows + row, planes, stride=rows), :]
-        middle = yy[pl.ds(8, planes), :]
-        ends = yy[pl.ds(7, planes), :] + yy[pl.ds(9, planes), :]
-        return ends + (middle + middle)
-
-    y_couples = {}
+        return sm[pl.ds(rows + row, planes, stride=rows), :]
 
     def y_couple(row):
-        if row not in y_couples:
-            value = coupling(row_smoothed(row + 1) - row_smoothed(row))
-            if row == -1:
-                value = value * jnp.where(has[(0, -1)], 1.0, 0.0)
-            y_couples[row] = value
-        return y_couples[row]
+        if isinstance(row, int) and row == -1:
+            middle = yy[pl.ds(8, planes), :]
+            ends = yy[pl.ds(7, planes), :] + yy[pl.ds(9, planes), :]
+            value = coupling(row_smoothed(0) - (ends + (middle + middle)))
+            return value * jnp.where(has[(0, -1)], 1.0, 0.0)
+        return coupling(row_smoothed(row + 1) - row_smoothed(row))
 
     def y_keep(row, onward, back, part):
         yw[row] = onward
@@ -337,16 +352,14 @@
             ysnd[k, pl.ds(q * y_chunk, y_chunk), :] = value[k * y_chunk : (k + 1) * y_chunk]
     exchange("lat", ysnd, yrcv, (ys_send, ys_recv), lat_total, lm)
 
-    z_couples = {}
+    def from_plane(plane):
+        return pl.ds(pl.multiple_of(plane * rows, rows), rows)
 
     def z_couple(plane):
-        if plane not in z_couples:
-            diff = sm[pl.ds((plane + 2) * rows, rows), :] - sm[pl.ds((plane + 1) * rows, rows), :]
-            value = coupling(diff)
-            if plane == -1:
-                value = value * jnp.where(has[(-1, 0)], 1.0, 0.0)
-            z_couples[plane] = value
-        return z_couples[plane]
+        value = coupling(sm[from_plane(plane + 2), :] - sm[from_plane(plane + 1), :])
+        if isinstance(plane, int) and plane == -1:
+            value = value * jnp.where(has[(-1, 0)], 1.0, 0.0)
+        return value
 
     def z_keep(plane, onward, back, part):
         zw[plane] = onward
@@ -355,16 +368,14 @@
 
     z_chunk = rows // depth_total
     results = eliminate(
-        0, planes, z_couple, lambda plane: vol[pl.ds(plane * rows, rows), :], z_keep
+        0, planes, z_couple, lambda plane: vol[from_plane(plane), :], z_keep
     )
     for q, value in enumerate(results):
         for k in range(depth_total):
             zsnd[k, pl.ds(q * z_chunk, z_chunk), :] = value[k * z_chunk : (k + 1) * z_chunk]
     exchange("depth", zsnd, zrcv, (zs_send, zs_recv), depth_total, dm)
 
-    for block in range(blocks):
-        where = pl.ds(block * tile, tile)
-        sm_t[where, :] = sm[pl.ds(rows + block * tile, tile), :].T
+    turn_tiles(sm, rows, sm_t)
     cells = tile // 8
     spread = blocks * 8
 
@@ -374,20 +385,12 @@
     def turn(field, by):
         return pltpu.roll(field.reshape(blocks, 8, tile), by, 1).reshape(spread, tile)
 
-    x_couples = {}
-
     def x_couple(cell):
-        if cell not in x_couples:
-            if cell == -1:
-                value = turn(x_couple(cells - 1), 1)
-            elif cell == cells - 1:
-                sub = lax.rem(lax.broadcasted_iota(jnp.int32, (spread, tile), 0), 8)
-                diff = turn(sm_t[x_at(0), :], 7) - sm_t[x_at(cell), :]
-                value = jnp.where(sub == 7, 0.0, coupling(diff))
-            else:
-                value = coupling(sm_t[x_at(cell + 1), :] - sm_t[x_at(cell), :])
-            x_couples[cell] = value
-        return x_couples[cell]
+        if isinstance(cell, int) and cell == -1:
+            sub = lax.rem(lax.broadcasted_iota(jnp.int32, (spread, tile), 0), 8)
+            before = turn(sm_t[x_at(cells - 1), :], 1)
+            return jnp.where(sub == 0, 0.0, coupling(sm_t[x_at(0), :] - before))
+        return coupling(sm_t[x_at(cell + 1), :] - sm_t[x_at(cell), :])
 
     def x_keep(cell, onward, back, part):
         xw[cell] = onward
@@ -418,9 +421,7 @@
         x_out[x_at(cell), :] = value
 
     substitute(0, cells, turn(last, 1), last, lambda c: (xw[c], xv[c], xg[c]), x_emit)
-    for block in range(blocks):
-        where = pl.ds(block * tile, tile)
-        out[where, :] = x_out[where, :].T
+    turn_tiles(x_out, 0, out)
 
     def reduce_and_return(axis, rcv, ret, fin, recv, sems, total, me, chunk):
         wait_all(rcv, recv, total)
@@ -446,7 +447,7 @@
     gather(zfin, zsep, depth_total, z_chunk)
 
     def z_emit(plane, value):
-        where = pl.ds(plane * rows, rows)
+        where = from_plane(plane)
         out[where, :] = out[where, :] + value
 
     substitute(
@@ -502,11 +503,11 @@
             vmem(2 * rows),
             vmem(2, 2, 8),
             vmem(cells),
-            vmem((planes + 1) * rows),
+            vmem((planes + 2) * rows),
             vmem(planes + 16),
             vmem(2, planes + 16),
             vmem(cells),
-            vmem(cells),
+            vmem(cells + 8),
             vmem(cells),
             vmem(columns // 8, cells * 8 // columns),
             vmem(columns // 8, cells * 8 // columns),

time: 19.7 us -> 19.9 us (1.010)
  Pallas kernels: 18.8 us -> 19.1 us
    pallas_call x1, Pallas kernels: 18.8 us -> 19.1 us  [shards(): pl.pallas_call(functools.partial(kernel, depth_total, lat_total, planes,...]
where the time goes in v5:
time: 19.9 us; the launch traced here: 19.8 us
  Pallas kernels  19.1 us (96%)
  local copies, waits for them, and re-layouts  0.71 us (4%)
    pallas_call x1, Pallas kernels, shards(): pl.pallas_call(functools.partial(kernel, depth_total, lat_total, planes,...  19.1 us
    unnamed x1, local copies, waits for them, and re-layouts  0.71 us

profile of v5, /device:TPU:0, one launch (start us, length us, event | category | flops | bytes accessed | tf_op | source)
XLA Modules:
  0.0 19.8 jit_solution(4043119915330388383)
XLA Ops:
  0.0 19.1 %shard_map.17 = f32[512,128]{1,0:T(8,128)S(1)} custom-call(f32[512,128]{1,0:T(8,128)} %bitcast.3), custom_call_target="tpu_custom_call" | custom-call | flops 26214400 | bytes 524288 | tf_op jit(solution)/shard_map/pallas_call | solution.py:491
  19.1 0.7 %copy.3 = f32[32,16,128]{2,1,0:T(8,128)} copy(f32[32,16,128]{2,1,0:T(8,128)S(1)} %bitcast.2) | data formatting | bytes 524288

commit v6 on v4

--- a/solution.py
+++ b/solution.py
@@ -127,6 +127,11 @@
     return values[::-1]
 
 
+def lat_solvers(lat_total):
+    solvers = max(lat_total // 2, 1)
+    return (lat_total - solvers) // 2, solvers
+
+
 def kernel(
     depth_total, lat_total, planes, rows,
     source, out,
@@ -153,15 +158,28 @@
     load.start()
 
     barrier = pltpu.get_barrier_semaphore()
+    first_solver, solvers = lat_solvers(lat_total)
+
+    def solves(index):
+        return jnp.logical_and(index >= first_solver, index < first_solver + solvers)
+
+    expected = jnp.int32(depth_total - 1)
     for step in range(1, lat_total):
-        pl.semaphore_signal(
-            barrier, inc=1, device_id=(dm, lax.rem(lm + step, lat_total)), device_id_type=MESH
+        other = lax.rem(lm + step, lat_total)
+        meets = jnp.logical_or(
+            jnp.logical_or(solves(lm), solves(other)),
+            jnp.logical_or(other == lm + 1, other == lm - 1),
         )
+        expected = expected + meets.astype(jnp.int32)
+
+        @pl.when(meets)
+        def _():
+            pl.semaphore_signal(barrier, inc=1, device_id=(dm, other), device_id_type=MESH)
+
     for step in range(1, depth_total):
         pl.semaphore_signal(
             barrier, inc=1, device_id=(lax.rem(dm + step, depth_total), lm), device_id_type=MESH
         )
-    expected = jnp.int32(lat_total + depth_total - 2)
     for dz, dy in corners:
         expected = expected + has[(dz, dy)].astype(jnp.int32)
 
@@ -328,14 +346,44 @@
         yv[row] = back
         yg[row] = part
 
-    y_chunk = planes // lat_total
+    y_chunk = planes // solvers
     results = eliminate(
         0, rows, y_couple, lambda row: vol[pl.ds(row, planes, stride=rows), :], y_keep
     )
     for q, value in enumerate(results):
-        for k in range(lat_total):
+        for k in range(solvers):
             ysnd[k, pl.ds(q * y_chunk, y_chunk), :] = value[k * y_chunk : (k + 1) * y_chunk]
-    exchange("lat", ysnd, yrcv, (ys_send, ys_recv), lat_total, lm)
+
+    def to_solver(k):
+        return pltpu.make_async_remote_copy(
+            src_ref=ysnd.at[k],
+            dst_ref=yrcv.at[lm],
+            send_sem=ys_send,
+            recv_sem=ys_recv,
+            device_id=(dm, first_solver + k),
+            device_id_type=MESH,
+        )
+
+    def from_solver(k):
+        return pltpu.make_async_remote_copy(
+            src_ref=yret.at[k],
+            dst_ref=yfin.at[lm - first_solver],
+            send_sem=yr_send,
+            recv_sem=yr_recv,
+            device_id=(dm, k),
+            device_id_type=MESH,
+        )
+
+    for k in range(solvers):
+
+        @pl.when(lm != first_solver + k)
+        def _():
+            to_solver(k).start()
+
+    @pl.when(solves(lm))
+    def _():
+        yrcv[lm] = ysnd[lm - first_solver]
+
 
     z_couples = {}
 
@@ -424,18 +472,32 @@
 
     def reduce_and_return(axis, rcv, ret, fin, recv, sems, total, me, chunk):
         wait_all(rcv, recv, total)
+        reduce_into(rcv, ret, total, chunk)
+        exchange(axis, ret, fin, sems, total, me)
+
+    def reduce_into(rcv, ret, total, chunk):
         values = solve_reduced(
             total, chunk, lambda k, q: rcv[k, pl.ds(q * chunk, chunk), :]
         )
         for k in range(total):
             ret[k, pl.ds(0, chunk), :] = values[k - 1] if k else jnp.zeros_like(values[0])
             ret[k, pl.ds(chunk, chunk), :] = values[k]
-        exchange(axis, ret, fin, sems, total, me)
-
-    y_sems = (yr_send, yr_recv)
+
     z_sems = (zr_send, zr_recv)
-    reduce_and_return("lat", yrcv, yret, yfin, ys_recv, y_sems, lat_total, lm, y_chunk)
     reduce_and_return("depth", zrcv, zret, zfin, zs_recv, z_sems, depth_total, dm, z_chunk)
+
+    @pl.when(solves(lm))
+    def _():
+        wait_all(yrcv, ys_recv, lat_total)
+        reduce_into(yrcv, yret, lat_total, y_chunk)
+        for k in sorted(range(lat_total), key=lambda k: -abs(2 * k + 1 - lat_total)):
+
+            @pl.when(lm != k)
+            def _():
+                from_solver(k).start()
+
+        yfin[lm - first_solver] = yret[lm]
+
 
     def gather(fin, sep, total, chunk):
         for k in range(total):
@@ -452,21 +514,32 @@
     substitute(
         0, planes, zsep[0], zsep[1], lambda p: (zw[p], zv[p], zg[p]), z_emit
     )
-    wait_all(yfin, yr_recv, lat_total)
-    gather(yfin, ysep, lat_total, y_chunk)
+
+    def wait_solvers(ref, sem):
+        @pl.when(solves(lm))
+        def _():
+            wait_all(ref, sem, solvers)
+
+        @pl.when(jnp.logical_not(solves(lm)))
+        def _():
+            wait_all(ref, sem, solvers + 1)
+
+    wait_solvers(yfin, yr_recv)
+    gather(yfin, ysep, solvers, y_chunk)
 
     def y_emit(row, value):
         where = pl.ds(row, planes, stride=rows)
         out[where, :] = (out[where, :] + value) * (1.0 / 3.0)
 
     substitute(0, rows, ysep[0], ysep[1], lambda r: (yw[r], yv[r], yg[r]), y_emit)
-    for ref, sem, total in (
-        (ysnd, ys_send, lat_total),
-        (yret, yr_send, lat_total),
-        (zsnd, zs_send, depth_total),
-        (zret, zr_send, depth_total),
-    ):
-        wait_all(ref, sem, total)
+    wait_all(zsnd, zs_send, depth_total)
+    wait_all(zret, zr_send, depth_total)
+    wait_solvers(ysnd, ys_send)
+
+    @pl.when(solves(lm))
+    def _():
+        wait_all(yret, yr_send, lat_total)
+
     for index, way in enumerate(ways):
 
         @pl.when(has[way])
@@ -476,7 +549,8 @@
 
 def shards(depth_total, lat_total, volume):
     planes, rows, columns = volume.shape
-    y_chunk = planes // lat_total
+    solvers = lat_solvers(lat_total)[1]
+    y_chunk = planes // solvers
     z_chunk = rows // depth_total
     f32 = jnp.float32
 
@@ -522,10 +596,10 @@
             vmem(depth_total, 2 * z_chunk),
             vmem(depth_total, 2 * z_chunk),
             vmem(2, rows),
-            vmem(lat_total, 5 * y_chunk),
+            vmem(solvers, 5 * y_chunk),
             vmem(lat_total, 5 * y_chunk),
             vmem(lat_total, 2 * y_chunk),
-            vmem(lat_total, 2 * y_chunk),
+            vmem(solvers, 2 * y_chunk),
             vmem(2, planes),
             pltpu.SemaphoreType.DMA,
             dma(8),

time: 19.7 us -> 18.7 us (0.949)
  Pallas kernels: 18.8 us -> 17.9 us
    pallas_call x1, Pallas kernels: 18.8 us -> 17.9 us  [shards(): pl.pallas_call(functools.partial(kernel, depth_total, lat_total, planes,...]
where the time goes in v6:
time: 18.7 us; the launch traced here: 18.6 us
  Pallas kernels  17.9 us (96%)
  local copies, waits for them, and re-layouts  0.71 us (4%)
    pallas_call x1, Pallas kernels, shards(): pl.pallas_call(functools.partial(kernel, depth_total, lat_total, planes,...  17.9 us
    unnamed x1, local copies, waits for them, and re-layouts  0.71 us

profile of v6, /device:TPU:0, one launch (start us, length us, event | category | flops | bytes accessed | tf_op | source)
XLA Modules:
  0.0 18.6 jit_solution(16515289521884982303)
XLA Ops:
  0.0 17.9 %shard_map.17 = f32[512,128]{1,0:T(8,128)S(1)} custom-call(f32[512,128]{1,0:T(8,128)} %bitcast.3), custom_call_target="tpu_custom_call" | custom-call | flops 26214400 | bytes 524288 | tf_op jit(solution)/shard_map/pallas_call | solution.py:564
  17.9 0.7 %copy.3 = f32[32,16,128]{2,1,0:T(8,128)} copy(f32[32,16,128]{2,1,0:T(8,128)S(1)} %bitcast.2) | data formatting | bytes 524288

commit v7 on v6

--- a/solution.py
+++ b/solution.py
@@ -105,26 +105,35 @@
             emit(start + step, value)
 
 
-def solve_reduced(count, rows, got):
-    excess = got(0, 3)
-    src = got(0, 4)
-    onwards, parts = [], []
-    for k in range(count - 1):
-        couple = got(k + 1, 2)
-        excess = excess + got(k + 1, 0)
-        src = src + got(k + 1, 1)
-        inverse = recip(excess + couple)
-        onward = couple * inverse
-        onwards.append(onward)
-        parts.append(src * inverse)
-        excess = got(k + 1, 3) + onward * excess
-        src = got(k + 1, 4) + onward * src
-    value = src * recip(excess)
-    values = [value]
-    for k in range(count - 2, -1, -1):
-        value = parts[k] + onwards[k] * value
-        values.append(value)
-    return values[::-1]
+def solve_reduced(count, got):
+    middle = count // 2
+    excess, src = [], []
+    for k in range(count):
+        more = k + 1 < count
+        excess.append(got(k, 3) + got(k + 1, 0) if more else got(k, 3))
+        src.append(got(k, 4) + got(k + 1, 1) if more else got(k, 4))
+    towards, parts = {}, {}
+
+    def fold(k, into):
+        couple = got(max(k, into), 2)
+        inverse = recip(excess[k] + couple)
+        towards[k] = couple * inverse
+        parts[k] = src[k] * inverse
+        excess[into] = excess[into] + towards[k] * excess[k]
+        src[into] = src[into] + towards[k] * src[k]
+
+    for step in range(middle):
+        fold(step, step + 1)
+        if count - 1 - step > middle:
+            fold(count - 1 - step, count - 2 - step)
+    values = {middle: src[middle] * recip(excess[middle])}
+    for step in range(1, middle + 1):
+        values[middle - step] = parts[middle - step] + towards[middle - step] * values[middle - step + 1]
+        if middle + step < count:
+            values[middle + step] = (
+                parts[middle + step] + towards[middle + step] * values[middle + step - 1]
+            )
+    return [values[k] for k in range(count)]
 
 
 def lat_solvers(lat_total):
@@ -445,6 +454,41 @@
     excess_low, src_low, couple, excess, src = eliminate(
         0, cells, x_couple, lambda cell: vol_t[x_at(cell), :], x_keep
     )
+    x_ends = (excess_low, src_low, couple, excess, src)
+
+    def reduce_and_return(axis, rcv, ret, fin, recv, sems, total, me, chunk):
+        wait_all(rcv, recv, total)
+        reduce_into(rcv, ret, total, chunk)
+        exchange(axis, ret, fin, sems, total, me)
+
+    def reduce_into(rcv, ret, total, chunk):
+        values = solve_reduced(total, lambda k, q: rcv[k, pl.ds(q * chunk, chunk), :])
+        for k in range(total):
+            ret[k, pl.ds(0, chunk), :] = values[k - 1] if k else jnp.zeros_like(values[0])
+            ret[k, pl.ds(chunk, chunk), :] = values[k]
+
+    z_sems = (zr_send, zr_recv)
+    reduce_and_return("depth", zrcv, zret, zfin, zs_recv, z_sems, depth_total, dm, z_chunk)
+
+    @pl.when(solves(lm))
+    def _():
+        wait_all(yrcv, ys_recv, lat_total)
+        reduce_into(yrcv, yret, lat_total, y_chunk)
+        for k in sorted(range(lat_total), key=lambda k: -abs(2 * k + 1 - lat_total)):
+
+            @pl.when(lm != k)
+            def _():
+                from_solver(k).start()
+
+        yfin[lm - first_solver] = yret[lm]
+
+
+    def gather(fin, sep, total, chunk):
+        for k in range(total):
+            for q in range(2):
+                sep[q, pl.ds(k * chunk, chunk), :] = fin[k, pl.ds(q * chunk, chunk), :]
+
+    excess_low, src_low, couple, excess, src = x_ends
     diag = excess + turn(excess_low, 7) + couple
     src = src + turn(src_low, 7)
     couple = turn(couple, 7)
@@ -469,40 +513,6 @@
     for block in range(blocks):
         where = pl.ds(block * tile, tile)
         out[where, :] = x_out[where, :].T
-
-    def reduce_and_return(axis, rcv, ret, fin, recv, sems, total, me, chunk):
-        wait_all(rcv, recv, total)
-        reduce_into(rcv, ret, total, chunk)
-        exchange(axis, ret, fin, sems, total, me)
-
-    def reduce_into(rcv, ret, total, chunk):
-        values = solve_reduced(
-            total, chunk, lambda k, q: rcv[k, pl.ds(q * chunk, chunk), :]
-        )
-        for k in range(total):
-            ret[k, pl.ds(0, chunk), :] = values[k - 1] if k else jnp.zeros_like(values[0])
-            ret[k, pl.ds(chunk, chunk), :] = values[k]
-
-    z_sems = (zr_send, zr_recv)
-    reduce_and_return("depth", zrcv, zret, zfin, zs_recv, z_sems, depth_total, dm, z_chunk)
-
-    @pl.when(solves(lm))
-    def _():
-        wait_all(yrcv, ys_recv, lat_total)
-        reduce_into(yrcv, yret, lat_total, y_chunk)
-        for k in sorted(range(lat_total), key=lambda k: -abs(2 * k + 1 - lat_total)):
-
-            @pl.when(lm != k)
-            def _():
-                from_solver(k).start()
-
-        yfin[lm - first_solver] = yret[lm]
-
-
-    def gather(fin, sep, total, chunk):
-        for k in range(total):
-            for q in range(2):
-                sep[q, pl.ds(k * chunk, chunk), :] = fin[k, pl.ds(q * chunk, chunk), :]
 
     wait_all(zfin, zr_recv, depth_total)
     gather(zfin, zsep, depth_total, z_chunk)

time: 18.7 us -> 18.7 us (level)
  no operation moved by 1% of the time
where the time goes in v7:
time: 18.7 us; the launch traced here: 18.5 us
  Pallas kernels  17.8 us (95%)
  local copies, waits for them, and re-layouts  0.71 us (4%)
    pallas_call x1, Pallas kernels, shards(): pl.pallas_call(functools.partial(kernel, depth_total, lat_total, planes,...  17.8 us
    unnamed x1, local copies, waits for them, and re-layouts  0.71 us

profile of v7, /device:TPU:0, one launch (start us, length us, event | category | flops | bytes accessed | tf_op | source)
XLA Modules:
  0.0 18.5 jit_solution(10834573872899672700)
XLA Ops:
  0.0 17.8 %shard_map.17 = f32[512,128]{1,0:T(8,128)S(1)} custom-call(f32[512,128]{1,0:T(8,128)} %bitcast.3), custom_call_target="tpu_custom_call" | custom-call | flops 26214400 | bytes 524288 | tf_op jit(solution)/shard_map/pallas_call | solution.py:574
  17.8 0.7 %copy.3 = f32[32,16,128]{2,1,0:T(8,128)} copy(f32[32,16,128]{2,1,0:T(8,128)S(1)} %bitcast.2) | data formatting | bytes 524288

commit v8 on v7

--- a/solution.py
+++ b/solution.py
@@ -145,6 +145,7 @@
     depth_total, lat_total, planes, rows,
     source, out,
     vol, pack_one, pack_two, yh_one, yh_two, zh_one, zh_two, cn, sm_x, sm, yy, nn,
+    vol_y, sm_y, part_y,
     vol_t, sm_t, x_out, xw, xv, xg, zw, zv, zg, yw, yv, yg,
     zsnd, zrcv, zret, zfin, zsep, ysnd, yrcv, yret, yfin, ysep,
     load_sem, halo_send, halo_recv, zs_send, zs_recv, zr_send, zr_recv,
@@ -257,11 +258,12 @@
             total = total if older is None else total + older
             sm[plane_at(plane - 1), :] = total if new is None else total + new
         older, old = old, new
-    tile = vol.shape[1]
-    blocks = planes * rows // tile
-    for block in range(blocks):
-        where = pl.ds(block * tile, tile)
-        vol_t[where, :] = vol[where, :].T
+    def row_at(row):
+        return pl.ds(row * planes, planes)
+
+    for row in range(rows):
+        vol_y[row_at(row), :] = vol[pl.ds(row, planes, stride=rows), :]
+        sm_y[row_at(row), :] = sm[pl.ds(rows + row, planes, stride=rows), :]
 
     for index, way in enumerate(ways):
         back = opposite[way]
@@ -289,7 +291,11 @@
     low_y = smooth_y(low_x)
     sm[plane_at(-1), :] = sm[plane_at(-1), :] + smooth_y(far_x) + (low_y + low_y)
     sm[plane_at(0), :] = sm[plane_at(0), :] + low_y
-    sm[plane_at(planes - 1), :] = sm[plane_at(planes - 1), :] + smooth_y(high_x)
+    high_y = smooth_y(high_x)
+    sm[plane_at(planes - 1), :] = sm[plane_at(planes - 1), :] + high_y
+    for plane, change in ((0, low_y), (planes - 1, high_y)):
+        where = pl.ds(plane, rows, stride=planes)
+        sm_y[where, :] = sm_y[where, :] + change
     low_tile = smooth_x(cn[0, 0])
     high_tile = smooth_x(cn[1, 0])
     far_row = smooth_x(yh_two[pl.ds(0, planes, stride=2), :])
@@ -314,7 +320,9 @@
         nn[side, pl.ds(8 + planes, 1), :] = after
         where = pl.ds(rows + edge, planes, stride=rows)
         ends = nn[side, pl.ds(7, planes), :] + nn[side, pl.ds(9, planes), :]
-        sm[where, :] = sm[where, :] + ends + (row + row)
+        change = ends + (row + row)
+        sm[where, :] = sm[where, :] + change
+        sm_y[row_at(edge), :] = sm_y[row_at(edge), :] + change
 
     def exchange(axis, src, dst, sems, total, me):
         for step in sorted(range(1, total), key=lambda step: abs(2 * step - total)):
@@ -334,8 +342,8 @@
         pltpu.make_async_copy(some, some, sem).wait()
 
     def row_smoothed(row):
-        if 0 <= row < rows:
-            return sm[pl.ds(rows + row, planes, stride=rows), :]
+        if row >= 0:
+            return sm_y[row_at(row), :]
         middle = yy[pl.ds(8, planes), :]
         ends = yy[pl.ds(7, planes), :] + yy[pl.ds(9, planes), :]
         return ends + (middle + middle)
@@ -357,7 +365,7 @@
 
     y_chunk = planes // solvers
     results = eliminate(
-        0, rows, y_couple, lambda row: vol[pl.ds(row, planes, stride=rows), :], y_keep
+        0, rows, y_couple, lambda row: vol_y[row_at(row), :], y_keep
     )
     for q, value in enumerate(results):
         for k in range(solvers):
@@ -419,8 +427,11 @@
             zsnd[k, pl.ds(q * z_chunk, z_chunk), :] = value[k * z_chunk : (k + 1) * z_chunk]
     exchange("depth", zsnd, zrcv, (zs_send, zs_recv), depth_total, dm)
 
+    tile = vol.shape[1]
+    blocks = planes * rows // tile
     for block in range(blocks):
         where = pl.ds(block * tile, tile)
+        vol_t[where, :] = vol[where, :].T
         sm_t[where, :] = sm[pl.ds(rows + block * tile, tile), :].T
     cells = tile // 8
     spread = blocks * 8
@@ -525,6 +536,9 @@
         0, planes, zsep[0], zsep[1], lambda p: (zw[p], zv[p], zg[p]), z_emit
     )
 
+    for row in range(rows):
+        part_y[row_at(row), :] = out[pl.ds(row, planes, stride=rows), :] * (1.0 / 3.0)
+
     def wait_solvers(ref, sem):
         @pl.when(solves(lm))
         def _():
@@ -538,8 +552,7 @@
     gather(yfin, ysep, solvers, y_chunk)
 
     def y_emit(row, value):
-        where = pl.ds(row, planes, stride=rows)
-        out[where, :] = (out[where, :] + value) * (1.0 / 3.0)
+        out[pl.ds(row, planes, stride=rows), :] = part_y[row_at(row), :] + value * (1.0 / 3.0)
 
     substitute(0, rows, ysep[0], ysep[1], lambda r: (yw[r], yv[r], yg[r]), y_emit)
     wait_all(zsnd, zs_send, depth_total)
@@ -589,6 +602,9 @@
             vmem((planes + 1) * rows),
             vmem(planes + 16),
             vmem(2, planes + 16),
+            vmem(cells),
+            vmem(cells),
+            vmem(cells),
             vmem(cells),
             vmem(cells),
             vmem(cells),

time: 18.7 us -> 18.6 us (level)
  no operation moved by 1% of the time
where the time goes in v8:
time: 18.6 us; the launch traced here: 18.4 us
  Pallas kernels  17.7 us (95%)
  local copies, waits for them, and re-layouts  0.71 us (4%)
    pallas_call x1, Pallas kernels, shards(): pl.pallas_call(functools.partial(kernel, depth_total, lat_total, planes,...  17.7 us
    unnamed x1, local copies, waits for them, and re-layouts  0.71 us

profile of v8, /device:TPU:0, one launch (start us, length us, event | category | flops | bytes accessed | tf_op | source)
XLA Modules:
  0.0 18.4 jit_solution(3953505332197290528)
XLA Ops:
  0.0 17.7 %shard_map.17 = f32[512,128]{1,0:T(8,128)S(1)} custom-call(f32[512,128]{1,0:T(8,128)} %bitcast.3), custom_call_target="tpu_custom_call" | custom-call | flops 26214400 | bytes 524288 | tf_op jit(solution)/shard_map/pallas_call | solution.py:587
  17.7 0.7 %copy.3 = f32[32,16,128]{2,1,0:T(8,128)} copy(f32[32,16,128]{2,1,0:T(8,128)S(1)} %bitcast.2) | data formatting | bytes 524288

commit v9 on v8

--- a/solution.py
+++ b/solution.py
@@ -226,7 +226,7 @@
             device_id_type=MESH,
         )
 
-    ways = [(0, -1), (0, 1), (-1, 0), (1, 0)] + corners
+    ways = [(0, -1), (0, 1)] + corners + [(-1, 0), (1, 0)]
     opposite = {way: ways.index((-way[0], -way[1])) for way in ways}
     for index, way in enumerate(ways):
 
@@ -265,64 +265,142 @@
         vol_y[row_at(row), :] = vol[pl.ds(row, planes, stride=rows), :]
         sm_y[row_at(row), :] = sm[pl.ds(rows + row, planes, stride=rows), :]
 
-    for index, way in enumerate(ways):
-        back = opposite[way]
-
-        @pl.when(has[way])
-        def _():
-            halo_copy(back, ways[back]).wait_recv()
-
-        @pl.when(jnp.logical_not(has[way]))
-        def _():
-            dz, dy = way
-            zi, yi = (dz + 1) // 2, (dy + 1) // 2
-            if dy == 0:
-                ref = zh_two if dz < 0 else zh_one
-                ref[...] = jnp.zeros(ref.shape, jnp.float32)
-            elif dz == 0:
-                ref = yh_two if dy < 0 else yh_one
-                ref[...] = jnp.zeros(ref.shape, jnp.float32)
+    def wait_halos(chosen):
+        for way in chosen:
+            back = opposite[way]
+
+            @pl.when(has[way])
+            def _():
+                halo_copy(back, ways[back]).wait_recv()
+
+            @pl.when(jnp.logical_not(has[way]))
+            def _():
+                dz, dy = way
+                zi, yi = (dz + 1) // 2, (dy + 1) // 2
+                if dy == 0:
+                    ref = zh_two if dz < 0 else zh_one
+                    ref[...] = jnp.zeros(ref.shape, jnp.float32)
+                elif dz == 0:
+                    ref = yh_two if dy < 0 else yh_one
+                    ref[...] = jnp.zeros(ref.shape, jnp.float32)
+                else:
+                    cn[zi, yi] = jnp.zeros(cn.shape[2:], jnp.float32)
+
+    y_chunk = planes // solvers
+
+    def row_smoothed(row, spans):
+        parts = []
+        for lo, hi in spans:
+            if row >= 0:
+                parts.append(sm_y[pl.ds(row * planes + lo, hi - lo), :])
             else:
-                cn[zi, yi] = jnp.zeros(cn.shape[2:], jnp.float32)
-
+                middle = yy[pl.ds(8 + lo, hi - lo), :]
+                ends = yy[pl.ds(7 + lo, hi - lo), :] + yy[pl.ds(9 + lo, hi - lo), :]
+                parts.append(ends + (middle + middle))
+        return jnp.concatenate(parts, axis=0)
+
+    def to_solver(k):
+        return pltpu.make_async_remote_copy(
+            src_ref=ysnd.at[k],
+            dst_ref=yrcv.at[lm],
+            send_sem=ys_send,
+            recv_sem=ys_recv,
+            device_id=(dm, first_solver + k),
+            device_id_type=MESH,
+        )
+
+    def eliminate_rows(spans):
+        couples = {}
+
+        def couple(row):
+            if row not in couples:
+                value = coupling(row_smoothed(row + 1, spans) - row_smoothed(row, spans))
+                if row == -1:
+                    value = value * jnp.where(has[(0, -1)], 1.0, 0.0)
+                couples[row] = value
+            return couples[row]
+
+        def source(row):
+            return jnp.concatenate(
+                [vol_y[pl.ds(row * planes + lo, hi - lo), :] for lo, hi in spans], axis=0
+            )
+
+        def keep(row, *values):
+            for ref, value in zip((yw, yv, yg), values):
+                base = 0
+                for lo, hi in spans:
+                    ref[row, pl.ds(lo, hi - lo), :] = value[base : base + hi - lo]
+                    base += hi - lo
+
+        results = eliminate(0, rows, couple, source, keep)
+        used = []
+        base = 0
+        for lo, hi in spans:
+            for plane in range(lo, hi, y_chunk):
+                k = plane // y_chunk
+                used.append(k)
+                for q, value in enumerate(results):
+                    ysnd[k, pl.ds(q * y_chunk, y_chunk), :] = value[base : base + y_chunk]
+                base += y_chunk
+        for k in used:
+
+            @pl.when(lm != first_solver + k)
+            def _():
+                to_solver(k).start()
+
+            @pl.when(lm == first_solver + k)
+            def _():
+                yrcv[lm] = ysnd[k]
+
+    wait_halos(ways[:2])
+    far_row = smooth_x(yh_two[pl.ds(0, planes, stride=2), :])
+    low_row = smooth_x(yh_two[pl.ds(1, planes, stride=2), :])
+    high_row = smooth_x(yh_one[...])
+    edge_row = sm_x[pl.ds(0, planes, stride=rows), :]
+    yy[pl.ds(8, planes), :] = (far_row + edge_row) + (low_row + low_row)
+    for side, edge, row in ((0, 0, low_row), (1, rows - 1, high_row)):
+        nn[side, pl.ds(8, planes), :] = row
+        nn[side, pl.ds(0, 8), :] = jnp.zeros((8, vol.shape[1]), jnp.float32)
+        nn[side, pl.ds(8 + planes, 8), :] = jnp.zeros((8, vol.shape[1]), jnp.float32)
+        where = pl.ds(rows + edge, planes, stride=rows)
+        ends = nn[side, pl.ds(7, planes), :] + nn[side, pl.ds(9, planes), :]
+        change = ends + (row + row)
+        sm[where, :] = sm[where, :] + change
+        sm_y[row_at(edge), :] = sm_y[row_at(edge), :] + change
+
+    eliminate_rows(((8, planes - 8),))
+
+    wait_halos(ways[2:])
     far_x = smooth_x(zh_two[pl.ds(0, rows), :])
     low_x = smooth_x(zh_two[pl.ds(rows, rows), :])
     high_x = smooth_x(zh_one[...])
     low_y = smooth_y(low_x)
-    sm[plane_at(-1), :] = sm[plane_at(-1), :] + smooth_y(far_x) + (low_y + low_y)
-    sm[plane_at(0), :] = sm[plane_at(0), :] + low_y
     high_y = smooth_y(high_x)
-    sm[plane_at(planes - 1), :] = sm[plane_at(planes - 1), :] + high_y
-    for plane, change in ((0, low_y), (planes - 1, high_y)):
-        where = pl.ds(plane, rows, stride=planes)
-        sm_y[where, :] = sm_y[where, :] + change
     low_tile = smooth_x(cn[0, 0])
     high_tile = smooth_x(cn[1, 0])
-    far_row = smooth_x(yh_two[pl.ds(0, planes, stride=2), :])
-    low_row = smooth_x(yh_two[pl.ds(1, planes, stride=2), :])
-    edge_row = sm_x[pl.ds(0, planes, stride=rows), :]
-    yy[pl.ds(8, planes), :] = (far_row + edge_row) + (low_row + low_row)
     for where, plane_x, far_one, near_one in (
         (7, low_x, low_tile[6:7], low_tile[7:8]),
         (8 + planes, high_x, high_tile[0:1], high_tile[1:2]),
     ):
         yy[pl.ds(where, 1), :] = (far_one + plane_x[0:1]) + (near_one + near_one)
-    low_side = (0, 0, low_row, low_tile[5:6], low_tile[7:8], high_tile[1:2])
+    low_side = (0, low_row, low_tile[5:6], low_tile[7:8], high_tile[1:2])
     low_tile = smooth_x(cn[0, 1])
     high_tile = smooth_x(cn[1, 1])
-    high_row = smooth_x(yh_one[...])
-    high_side = (1, rows - 1, high_row, low_tile[6:7], low_tile[7:8], high_tile[0:1])
-    for side, edge, row, two_before, before, after in (low_side, high_side):
+    high_side = (rows - 1, high_row, low_tile[6:7], low_tile[7:8], high_tile[0:1])
+    sm[plane_at(-1), :] = sm[plane_at(-1), :] + smooth_y(far_x) + (low_y + low_y)
+    for edge, row, two_before, before, after in (low_side, high_side):
         where = pl.ds(edge, 1)
         sm[where, :] = sm[where, :] + row[0:1] + two_before + (before + before)
-        nn[side, pl.ds(8, planes), :] = row
-        nn[side, pl.ds(7, 1), :] = before
-        nn[side, pl.ds(8 + planes, 1), :] = after
-        where = pl.ds(rows + edge, planes, stride=rows)
-        ends = nn[side, pl.ds(7, planes), :] + nn[side, pl.ds(9, planes), :]
-        change = ends + (row + row)
-        sm[where, :] = sm[where, :] + change
-        sm_y[row_at(edge), :] = sm_y[row_at(edge), :] + change
+        for plane, change in ((0, before), (planes - 1, after)):
+            where = pl.ds((plane + 1) * rows + edge, 1)
+            sm[where, :] = sm[where, :] + change
+            where = pl.ds(edge * planes + plane, 1)
+            sm_y[where, :] = sm_y[where, :] + change
+    for plane, change in ((0, low_y), (planes - 1, high_y)):
+        sm[plane_at(plane), :] = sm[plane_at(plane), :] + change
+        where = pl.ds(plane, rows, stride=planes)
+        sm_y[where, :] = sm_y[where, :] + change
+    eliminate_rows(((0, 8), (planes - 8, planes)))
 
     def exchange(axis, src, dst, sems, total, me):
         for step in sorted(range(1, total), key=lambda step: abs(2 * step - total)):
@@ -341,46 +419,6 @@
         some = ref.at[pl.ds(0, total - 1)]
         pltpu.make_async_copy(some, some, sem).wait()
 
-    def row_smoothed(row):
-        if row >= 0:
-            return sm_y[row_at(row), :]
-        middle = yy[pl.ds(8, planes), :]
-        ends = yy[pl.ds(7, planes), :] + yy[pl.ds(9, planes), :]
-        return ends + (middle + middle)
-
-    y_couples = {}
-
-    def y_couple(row):
-        if row not in y_couples:
-            value = coupling(row_smoothed(row + 1) - row_smoothed(row))
-            if row == -1:
-                value = value * jnp.where(has[(0, -1)], 1.0, 0.0)
-            y_couples[row] = value
-        return y_couples[row]
-
-    def y_keep(row, onward, back, part):
-        yw[row] = onward
-        yv[row] = back
-        yg[row] = part
-
-    y_chunk = planes // solvers
-    results = eliminate(
-        0, rows, y_couple, lambda row: vol_y[row_at(row), :], y_keep
-    )
-    for q, value in enumerate(results):
-        for k in range(solvers):
-            ysnd[k, pl.ds(q * y_chunk, y_chunk), :] = value[k * y_chunk : (k + 1) * y_chunk]
-
-    def to_solver(k):
-        return pltpu.make_async_remote_copy(
-            src_ref=ysnd.at[k],
-            dst_ref=yrcv.at[lm],
-            send_sem=ys_send,
-            recv_sem=ys_recv,
-            device_id=(dm, first_solver + k),
-            device_id_type=MESH,
-        )
-
     def from_solver(k):
         return pltpu.make_async_remote_copy(
             src_ref=yret.at[k],
@@ -390,17 +428,6 @@
             device_id=(dm, k),
             device_id_type=MESH,
         )
-
-    for k in range(solvers):
-
-        @pl.when(lm != first_solver + k)
-        def _():
-            to_solver(k).start()
-
-    @pl.when(solves(lm))
-    def _():
-        yrcv[lm] = ysnd[lm - first_solver]
-
 
     z_couples = {}
 

time: 18.6 us -> 18.1 us (0.973)
  Pallas kernels: 17.7 us -> 17.2 us
    pallas_call x1, Pallas kernels: 17.7 us -> 17.2 us  [shards(): pl.pallas_call(functools.partial(kernel, depth_total, lat_total, planes,...]
where the time goes in v9:
time: 18.1 us; the launch traced here: 18 us
  Pallas kernels  17.2 us (95%)
  local copies, waits for them, and re-layouts  0.71 us (4%)
    pallas_call x1, Pallas kernels, shards(): pl.pallas_call(functools.partial(kernel, depth_total, lat_total, planes,...  17.2 us
    unnamed x1, local copies, waits for them, and re-layouts  0.71 us

profile of v9, /device:TPU:0, one launch (start us, length us, event | category | flops | bytes accessed | tf_op | source)
XLA Modules:
  0.0 18.0 jit_solution(2093964710256360427)
XLA Ops:
  0.0 17.2 %shard_map.17 = f32[512,128]{1,0:T(8,128)S(1)} custom-call(f32[512,128]{1,0:T(8,128)} %bitcast.3), custom_call_target="tpu_custom_call" | custom-call | flops 26214400 | bytes 524288 | tf_op jit(solution)/shard_map/pallas_call | solution.py:614
  17.3 0.7 %copy.3 = f32[32,16,128]{2,1,0:T(8,128)} copy(f32[32,16,128]{2,1,0:T(8,128)S(1)} %bitcast.2) | data formatting | bytes 524288

commit v10 on v9

--- a/solution.py
+++ b/solution.py
@@ -12,6 +12,7 @@
 MESH = pl.DeviceIdType.MESH
 SCALE = (64.0 * LAMBDA) ** 2
 LEAF = 8
+ROW_LEAF = 4
 
 
 def recip(value):
@@ -31,12 +32,12 @@
     return (before + after) + (field + field)
 
 
-def eliminate(lo, hi, couple, source, keep):
-    starts = list(range(lo, hi, LEAF))
+def eliminate(lo, hi, leaf, couple, source, keep):
+    starts = list(range(lo, hi, leaf))
     state = []
     for start in starts:
         state.append([1.0, couple(start - 1), source(start), None, None])
-    for step in range(LEAF - 1):
+    for step in range(leaf - 1):
         for part, start in enumerate(starts):
             excess, fill, src, excess_low, src_low = state[part]
             cell = start + step
@@ -54,7 +55,7 @@
                 add_excess if excess_low is None else excess_low + add_excess,
                 add_src if src_low is None else src_low + add_src,
             ]
-    blocks = [(start, start + LEAF, part) for start, part in zip(starts, state)]
+    blocks = [(start, start + leaf, part) for start, part in zip(starts, state)]
     while len(blocks) > 1:
         merged = []
         for first, second in zip(blocks[::2], blocks[1::2]):
@@ -84,11 +85,11 @@
     return el, sl, f, e, s
 
 
-def substitute(lo, hi, before, last, load, emit):
+def substitute(lo, hi, leaf, before, last, load, emit):
     known = {lo - 1: before, hi - 1: last}
     emit(hi - 1, last)
     size = hi - lo
-    while size > LEAF:
+    while size > leaf:
         for start in range(lo, hi, size):
             middle = start + size // 2 - 1
             onward, back, part = load(middle)
@@ -96,9 +97,9 @@
             known[middle] = value
             emit(middle, value)
         size = size // 2
-    current = {start: known[start + LEAF - 1] for start in range(lo, hi, LEAF)}
-    for step in range(LEAF - 2, -1, -1):
-        for start in range(lo, hi, LEAF):
+    current = {start: known[start + leaf - 1] for start in range(lo, hi, leaf)}
+    for step in range(leaf - 2, -1, -1):
+        for start in range(lo, hi, leaf):
             onward, back, part = load(start + step)
             value = part + back * known[start - 1] + onward * current[start]
             current[start] = value
@@ -332,7 +333,7 @@
                     ref[row, pl.ds(lo, hi - lo), :] = value[base : base + hi - lo]
                     base += hi - lo
 
-        results = eliminate(0, rows, couple, source, keep)
+        results = eliminate(0, rows, ROW_LEAF, couple, source, keep)
         used = []
         base = 0
         for lo, hi in spans:
@@ -447,7 +448,7 @@
 
     z_chunk = rows // depth_total
     results = eliminate(
-        0, planes, z_couple, lambda plane: vol[pl.ds(plane * rows, rows), :], z_keep
+        0, planes, LEAF, z_couple, lambda plane: vol[pl.ds(plane * rows, rows), :], z_keep
     )
     for q, value in enumerate(results):
         for k in range(depth_total):
@@ -490,7 +491,7 @@
         xg[cell] = part
 
     excess_low, src_low, couple, excess, src = eliminate(
-        0, cells, x_couple, lambda cell: vol_t[x_at(cell), :], x_keep
+        0, cells, LEAF, x_couple, lambda cell: vol_t[x_at(cell), :], x_keep
     )
     x_ends = (excess_low, src_low, couple, excess, src)
 
@@ -547,7 +548,7 @@
     def x_emit(cell, value):
         x_out[x_at(cell), :] = value
 
-    substitute(0, cells, turn(last, 1), last, lambda c: (xw[c], xv[c], xg[c]), x_emit)
+    substitute(0, cells, LEAF, turn(last, 1), last, lambda c: (xw[c], xv[c], xg[c]), x_emit)
     for block in range(blocks):
         where = pl.ds(block * tile, tile)
         out[where, :] = x_out[where, :].T
@@ -560,7 +561,7 @@
         out[where, :] = out[where, :] + value
 
     substitute(
-        0, planes, zsep[0], zsep[1], lambda p: (zw[p], zv[p], zg[p]), z_emit
+        0, planes, LEAF, zsep[0], zsep[1], lambda p: (zw[p], zv[p], zg[p]), z_emit
     )
 
     for row in range(rows):
@@ -581,7 +582,7 @@
     def y_emit(row, value):
         out[pl.ds(row, planes, stride=rows), :] = part_y[row_at(row), :] + value * (1.0 / 3.0)
 
-    substitute(0, rows, ysep[0], ysep[1], lambda r: (yw[r], yv[r], yg[r]), y_emit)
+    substitute(0, rows, ROW_LEAF, ysep[0], ysep[1], lambda r: (yw[r], yv[r], yg[r]), y_emit)
     wait_all(zsnd, zs_send, depth_total)
     wait_all(zret, zr_send, depth_total)
     wait_solvers(ysnd, ys_send)

time: 18.1 us -> 18.1 us (level)
  no operation moved by 1% of the time
where the time goes in v10:
time: 18.1 us; the launch traced here: 17.9 us
  Pallas kernels  17.2 us (95%)
  local copies, waits for them, and re-layouts  0.71 us (4%)
    pallas_call x1, Pallas kernels, shards(): pl.pallas_call(functools.partial(kernel, depth_total, lat_total, planes,...  17.2 us
    unnamed x1, local copies, waits for them, and re-layouts  0.71 us

profile of v10, /device:TPU:0, one launch (start us, length us, event | category | flops | bytes accessed | tf_op | source)
XLA Modules:
  0.0 17.9 jit_solution(7237671678086385525)
XLA Ops:
  0.0 17.2 %shard_map.17 = f32[512,128]{1,0:T(8,128)S(1)} custom-call(f32[512,128]{1,0:T(8,128)} %bitcast.3), custom_call_target="tpu_custom_call" | custom-call | flops 26214400 | bytes 524288 | tf_op jit(solution)/shard_map/pallas_call | solution.py:615
  17.2 0.7 %copy.3 = f32[32,16,128]{2,1,0:T(8,128)} copy(f32[32,16,128]{2,1,0:T(8,128)S(1)} %bitcast.2) | data formatting | bytes 524288

commit v11 on v10

--- a/solution.py
+++ b/solution.py
@@ -455,6 +455,38 @@
             zsnd[k, pl.ds(q * z_chunk, z_chunk), :] = value[k * z_chunk : (k + 1) * z_chunk]
     exchange("depth", zsnd, zrcv, (zs_send, zs_recv), depth_total, dm)
 
+    def reduce_and_return(axis, rcv, ret, fin, recv, sems, total, me, chunk):
+        wait_all(rcv, recv, total)
+        reduce_into(rcv, ret, total, chunk)
+        exchange(axis, ret, fin, sems, total, me)
+
+    def reduce_into(rcv, ret, total, chunk):
+        values = solve_reduced(total, lambda k, q: rcv[k, pl.ds(q * chunk, chunk), :])
+        for k in range(total):
+            ret[k, pl.ds(0, chunk), :] = values[k - 1] if k else jnp.zeros_like(values[0])
+            ret[k, pl.ds(chunk, chunk), :] = values[k]
+
+    z_sems = (zr_send, zr_recv)
+    reduce_and_return("depth", zrcv, zret, zfin, zs_recv, z_sems, depth_total, dm, z_chunk)
+
+    @pl.when(solves(lm))
+    def _():
+        wait_all(yrcv, ys_recv, lat_total)
+        reduce_into(yrcv, yret, lat_total, y_chunk)
+        for k in sorted(range(lat_total), key=lambda k: -abs(2 * k + 1 - lat_total)):
+
+            @pl.when(lm != k)
+            def _():
+                from_solver(k).start()
+
+        yfin[lm - first_solver] = yret[lm]
+
+
+    def gather(fin, sep, total, chunk):
+        for k in range(total):
+            for q in range(2):
+                sep[q, pl.ds(k * chunk, chunk), :] = fin[k, pl.ds(q * chunk, chunk), :]
+
     tile = vol.shape[1]
     blocks = planes * rows // tile
     for block in range(blocks):
@@ -493,41 +525,6 @@
     excess_low, src_low, couple, excess, src = eliminate(
         0, cells, LEAF, x_couple, lambda cell: vol_t[x_at(cell), :], x_keep
     )
-    x_ends = (excess_low, src_low, couple, excess, src)
-
-    def reduce_and_return(axis, rcv, ret, fin, recv, sems, total, me, chunk):
-        wait_all(rcv, recv, total)
-        reduce_into(rcv, ret, total, chunk)
-        exchange(axis, ret, fin, sems, total, me)
-
-    def reduce_into(rcv, ret, total, chunk):
-        values = solve_reduced(total, lambda k, q: rcv[k, pl.ds(q * chunk, chunk), :])
-        for k in range(total):
-            ret[k, pl.ds(0, chunk), :] = values[k - 1] if k else jnp.zeros_like(values[0])
-            ret[k, pl.ds(chunk, chunk), :] = values[k]
-
-    z_sems = (zr_send, zr_recv)
-    reduce_and_return("depth", zrcv, zret, zfin, zs_recv, z_sems, depth_total, dm, z_chunk)
-
-    @pl.when(solves(lm))
-    def _():
-        wait_all(yrcv, ys_recv, lat_total)
-        reduce_into(yrcv, yret, lat_total, y_chunk)
-        for k in sorted(range(lat_total), key=lambda k: -abs(2 * k + 1 - lat_total)):
-
-            @pl.when(lm != k)
-            def _():
-                from_solver(k).start()
-
-        yfin[lm - first_solver] = yret[lm]
-
-
-    def gather(fin, sep, total, chunk):
-        for k in range(total):
-            for q in range(2):
-                sep[q, pl.ds(k * chunk, chunk), :] = fin[k, pl.ds(q * chunk, chunk), :]
-
-    excess_low, src_low, couple, excess, src = x_ends
     diag = excess + turn(excess_low, 7) + couple
     src = src + turn(src_low, 7)
     couple = turn(couple, 7)

time: 18.1 us -> 18.1 us (level)
  no operation moved by 1% of the time
where the time goes in v11:
time: 18.1 us; the launch traced here: 17.9 us
  Pallas kernels  17.2 us (95%)
  local copies, waits for them, and re-layouts  0.71 us (4%)
    pallas_call x1, Pallas kernels, shards(): pl.pallas_call(functools.partial(kernel, depth_total, lat_total, planes,...  17.2 us
    unnamed x1, local copies, waits for them, and re-layouts  0.71 us

profile of v11, /device:TPU:0, one launch (start us, length us, event | category | flops | bytes accessed | tf_op | source)
XLA Modules:
  0.0 17.9 jit_solution(11523305920286964618)
XLA Ops:
  0.0 17.2 %shard_map.17 = f32[512,128]{1,0:T(8,128)S(1)} custom-call(f32[512,128]{1,0:T(8,128)} %bitcast.3), custom_call_target="tpu_custom_call" | custom-call | flops 26214400 | bytes 524288 | tf_op jit(solution)/shard_map/pallas_call | solution.py:612
  17.2 0.7 %copy.3 = f32[32,16,128]{2,1,0:T(8,128)} copy(f32[32,16,128]{2,1,0:T(8,128)S(1)} %bitcast.2) | data formatting | bytes 524288
